TPU v7x, 128 devices: a whole 4x4x4 slice. The times are simulated.
128 devices in a mesh: req: 8 (over y, core), sp: 16 (over z, x).
Axes of the slice: x: 4, y: 4, z: 4, core: 2. Of those that a mesh axis runs over, the one named last changes fastest.
Arguments:
- hidden: bfloat16 [8, 4096, 3072], P('req', 'sp'), may hold values from -6 to 6
- latent_query_key_value: bfloat16 [8, 4096, 3, 2048], P('req', 'sp'), may hold values from -6 to 6
- features: bfloat16 [64, 128, 1152], P('req', 'sp'), may hold values from -6 to 6
- image_request: int32 [64, 1], P('req'), may hold values from 0 to 7; in each aligned block of 8 rows (0 to 7, 8 to 15, ...) at most 2 rows name the same one
- image_key_weight: bfloat16 [1152, 2048], P(None, 'sp'), may hold values from -0.1875 to 0.1875
- image_value_weight: bfloat16 [1152, 2048], P(None, 'sp'), may hold values from -0.1875 to 0.1875
- caller_lowfactor_index: int32 [8], replicated, may hold values from 0 to 15
- request_rank: int32 [8], replicated, may hold values from 16 to 64
- lowfactor_reducing_matrix: bfloat16 [16, 3072, 64], P('req'), may hold values from -0.109375 to 0.109375
- lowfactor_expanding_matrix: bfloat16 [16, 64, 2048], P('req'), may hold values from -0.75 to 0.75
Outputs:
- attended: bfloat16 [8, 4096, 2048], P('req', 'sp')
Inputs may be any that keep to these rules, and one draw needn't show every extreme that they name: `image_request`: in each block of 8 images of one index of req, at most 2 belong to one request; every request owns at least one image.
All inputs are finite; a program needn't handle non-finite values.
Results may differ from a plain program's by a relative error of at most 0.0093.
Values may be sent and summed in bfloat16 or wider, within the bound.
No kernel may reach another device: no remote copies, remote signals or barrier semaphores. Data moves between devices by JAX's collectives and lax.ppermute only.
A program may use at most 128 MiB of HBM per device.

v0:
```python
import math

import jax
import jax.numpy as jnp
from jax import lax
from jax.sharding import PartitionSpec as P

HD = 128
CAP = 2


adapter_alpha = 16.0
ip_scale = 1.0


def softmax_apply(query_block, key_rows, value_rows, key_valid):
    scores = jnp.einsum(
        "qhd,khd->hqk", query_block, key_rows, preferred_element_type=jnp.float32
    ) * HD ** (-0.5)
    if key_valid is not None:
        scores = jnp.where(key_valid[None, None, :], scores, -1e30)
    row_max = jnp.max(scores, axis=-1, keepdims=True)
    weights = jnp.exp(scores - row_max)
    weights = (weights / jnp.sum(weights, axis=-1, keepdims=True)).astype(jnp.bfloat16)
    return jnp.einsum("hqk,khd->qhd", weights, value_rows, preferred_element_type=jnp.float32)


def shards(
    hidden,
    latent_query_key_value,
    features,
    image_request,
    image_key_weight,
    image_value_weight,
    caller_lowfactor_index,
    request_rank,
    lowfactor_reducing_matrix,
    lowfactor_expanding_matrix,
):
    groups = lax.axis_size("req")
    group_position = lax.axis_index("req")
    adapter_choice = caller_lowfactor_index[group_position]
    adapter_rank_value = request_rank[group_position]
    bank_down, bank_up = (
        lax.all_gather(lowfactor_reducing_matrix, "req", axis=0, tiled=True),
        lax.all_gather(lowfactor_expanding_matrix, "req", axis=0, tiled=True),
    )
    pick_adapter = (jnp.arange(bank_down.shape[0]) == adapter_choice).astype(jnp.bfloat16)
    adapt_down = jnp.einsum(
        "a,adr->dr", pick_adapter, bank_down, preferred_element_type=jnp.float32
    ).astype(jnp.bfloat16)
    adapt_up = jnp.einsum(
        "a,arc->rc", pick_adapter, bank_up, preferred_element_type=jnp.float32
    ).astype(jnp.bfloat16)
    rank_activations = jnp.dot(hidden[0], adapt_down, preferred_element_type=jnp.float32)
    rank_activations = jnp.where(
        jnp.arange(rank_activations.shape[1])[None, :] < adapter_rank_value, rank_activations, 0.0
    ).astype(jnp.bfloat16)
    query_update = jnp.dot(rank_activations, adapt_up, preferred_element_type=jnp.float32)
    query_row_block = (
        latent_query_key_value[0, :, 0].astype(jnp.float32)
        + adapter_alpha / adapter_rank_value.astype(jnp.float32) * query_update
    ).astype(jnp.bfloat16)
    stacked = jnp.stack(
        [query_row_block, latent_query_key_value[0, :, 1], latent_query_key_value[0, :, 2]]
    )
    head_layout = lax.all_to_all(stacked, "sp", split_axis=2, concat_axis=1, tiled=True)
    owners = image_request[:, 0]
    local_images = owners.shape[0]
    matches = (owners[:, None] == owners[None, :]).astype(jnp.int32)
    slot_of = jnp.sum(jnp.tril(matches, -1), axis=1)
    placing = (owners[None, None, :] == jnp.arange(groups)[:, None, None]) & (
        slot_of[None, None, :] == jnp.arange(CAP)[None, :, None]
    )
    shard_tokens = features.shape[1]
    enc_width = features.shape[2]
    slot_rows = jnp.dot(
        placing.astype(jnp.bfloat16).reshape(groups * CAP, local_images),
        features.reshape(local_images, shard_tokens * enc_width),
        preferred_element_type=jnp.float32,
    )
    slot_rows = slot_rows.astype(jnp.bfloat16).reshape(groups, CAP, shard_tokens, enc_width)
    slot_flags = jnp.sum(placing.astype(jnp.float32), axis=2).astype(jnp.bfloat16)
    got_rows, got_flags = (
        lax.all_to_all(slot_rows, "req", split_axis=0, concat_axis=0, tiled=True),
        lax.all_to_all(slot_flags, "req", split_axis=0, concat_axis=0, tiled=True),
    )
    slot_count = groups * CAP
    got_rows = got_rows.reshape(slot_count, shard_tokens, enc_width)
    slot_valid = got_flags.reshape(slot_count) > 0.5
    head_cols = head_layout.shape[2]
    both_weights = jnp.concatenate([image_key_weight, image_value_weight], axis=1)
    piece = lax.all_gather(got_rows, "sp", axis=1, tiled=True)
    piece_tokens = piece.shape[1]
    product = jnp.dot(
        piece.reshape(slot_count * piece_tokens, enc_width),
        both_weights,
        preferred_element_type=jnp.float32,
    )
    image_kv = product.astype(jnp.bfloat16).reshape(slot_count, piece_tokens, 2, head_cols)
    heads_here = head_cols // HD
    img_keys = image_kv[:, :, 0].reshape(-1, heads_here, HD)
    img_vals = image_kv[:, :, 1].reshape(-1, heads_here, HD)
    token_valid = jnp.repeat(slot_valid, image_kv.shape[1])
    seq_len = head_layout.shape[1]
    own_query = head_layout[0].reshape(seq_len, heads_here, HD)
    own_keys = head_layout[1].reshape(seq_len, heads_here, HD)
    own_vals = head_layout[2].reshape(seq_len, heads_here, HD)
    block_rows = math.gcd(seq_len, 512)
    block_count = seq_len // block_rows

    def one_block(query_block):
        own = softmax_apply(query_block, own_keys, own_vals, None)
        image = softmax_apply(query_block, img_keys, img_vals, token_valid)
        return (own + ip_scale * image).astype(jnp.bfloat16)

    blocks_out = lax.map(one_block, own_query.reshape(block_count, block_rows, heads_here, HD))
    per_heads = blocks_out.reshape(seq_len, head_cols)
    attended = lax.all_to_all(per_heads, "sp", split_axis=0, concat_axis=1, tiled=True)
    return attended[None]


def solution(mesh):
    placed = (
        P("req", "sp", None),
        P("req", "sp", None, None),
        P("req", "sp", None),
        P("req", None),
        P(None, "sp"),
        P(None, "sp"),
        P(),
        P(),
        P("req", None, None),
        P("req", None, None),
    )
    return jax.shard_map(
        shards, mesh=mesh, in_specs=placed, out_specs=P("req", "sp", None), check_vma=False
    )
```

profile of v0, /device:TPU:0, one launch (start us, length us, event | category | flops | bytes accessed | tf_op | source)
XLA Modules:
  0.0 310.9 jit_solution(12746022659489054706)
XLA Ops:
  11.0 12.3 %all_to_all.42 = bf16[8,2,8,1152]{3,2,1,0:T(8,128)(2,1)} all-to-all(bf16[8,2,8,1152]{3,2,1,0:T(8,128)(2,1)S(1)} %bitcast.119), channel_id=1, replica_groups=mesh['req'=8,'sp'=16] {'req'}, dimensions={0} | all-to-all | bytes 589824 | tf_op jit(solution)/shard_map/all_to_all | solution.py:85
  24.1 3.3 %all-to-all-start.1 = ((bf16[8,1,2]{2,1,0:T(2,128)(2,1)}), bf16[8,1,2]{2,1,0:T(2,128)(2,1)S(1)}, u32[]{:S(2)}, u32[]{:S(2)}) async-start(bf16[8,1,2]{2,1,0:T(2,128)(2,1)} %copy.52), calls=%async_computation.1 | async-start | bytes 8192 | tf_op jit(solution)/shard_map/all_to_all | solution.py:86
  31.3 3.2 %slice_bitcast_fusion.1 = (bf16[1,256,2048]{2,1,0:T(8,128)(2,1)}, bf16[1,256,2048]{2,1,0:T(8,128)(2,1)}) fusion(bf16[1,256,3,2048]{3,1,2,0:T(8,128)(2,1)} %param.13), kind=kLoop, calls=%fused_computation.49 | loop fusion | bytes 4194304 | tf_op jit(solution)/shard_map/stack;squeeze | solution.py:64
  34.5 9.3 %all-gather.6.cloned.1.call-done = bf16[16,64,2048]{2,1,0:T(8,128)(2,1)} async-done(((bf16[2,64,2048]{2,1,0:T(8,128)(2,1)}), bf16[16,64,2048]{2,1,0:T(8,128)(2,1)}) %all-gather.6.cloned.1.call-update) | async-done | bytes 4194320 | tf_op jit(solution)/shard_map/all_gather | solution.py:46
  43.7 8.4 %fusion.28 = bf16[1,64,2048]{2,0,1:T(2,128)(2,1)} fusion(bf16[16,64,2048]{2,1,0:T(8,128)(2,1)} %all-gather.6.cloned.1.call-done, s32[]{:T(128)} %bitcast.2), kind=kOutput, calls=%fused_computation.35 | convolution fusion | flops 4194320 | bytes 4456452 | tf_op jit(solution)/shard_map/a,arc->rc/dot_general | solution.py:52
  52.1 34.2 %all-gather.4.cloned.1.call-done = bf16[16,3072,64]{1,2,0:T(8,128)(2,1)} async-done(((bf16[2,3072,64]{1,2,0:T(8,128)(2,1)}), bf16[16,3072,64]{1,2,0:T(8,128)(2,1)}) %all-gather.4.cloned.1.call-update) | async-done | bytes 6291472 | tf_op jit(solution)/shard_map/all_gather | solution.py:45
  86.3 10.7 %fusion.26 = bf16[1,3072,64]{1,0,2:T(2,128)(2,1)S(1)} fusion(bf16[16,3072,64]{1,2,0:T(8,128)(2,1)} %all-gather.4.cloned.1.call-done, s32[]{:T(128)} %bitcast.2), kind=kOutput, calls=%fused_computation.33 | convolution fusion | flops 6291472 | bytes 6684676 | tf_op jit(solution)/shard_map/a,adr->dr/dot_general | solution.py:49
  97.8 3.0 fusion.32
  100.8 3.6 %pad_maximum_fusion = bf16[3,256,2048]{2,1,0:T(8,128)(2,1)} fusion(bf16[1,256,2048]{2,1,0:T(8,128)(2,1)} %get-tuple-element.133, bf16[1,256,2048]{2,1,0:T(8,128)(2,1)} %get-tuple-element.132, bf16[1,256,2048]{2,1,0:T(8,128)(2,1)S(1)} %fusion.32), kind=kLoop, calls=%fused_computation.37 | loop fusion | flops 3145728 | bytes 6291456 | tf_op jit(solution)/shard_map/stack | solution.py:64
  104.5 7.2 %copy.44 = bf16[3,256,2048]{1,0,2:T(4,128)(2,1)} copy(bf16[3,256,2048]{2,1,0:T(8,128)(2,1)} %pad_maximum_fusion) | data formatting | bytes 6291456 | tf_op jit(solution)/shard_map/stack | solution.py:64
  111.7 7.1 %all-to-all-start = ((bf16[3,256,2048]{1,0,2:T(4,128)(2,1)}), bf16[3,256,2048]{1,0,2:T(4,128)(2,1)}, u32[]{:S(2)}, u32[]{:S(2)}) async-start(bf16[3,256,2048]{1,0,2:T(4,128)(2,1)} %copy.44), calls=%async_computation | async-start | bytes 8388608 | tf_op jit(solution)/shard_map/all_to_all | solution.py:67
  118.9 67.2 %all-gather.8.cloned.1.call-done = bf16[16,128,1152]{2,1,0:T(8,128)(2,1)} async-done(((bf16[16,8,1152]{2,1,0:T(8,128)(2,1)}), bf16[16,128,1152]{2,1,0:T(8,128)(2,1)}) %all-gather.8.cloned.1.call-update) | async-done | bytes 4718608 | tf_op jit(solution)/shard_map/all_gather | solution.py:93
  186.1 3.9 %convolution_convert_fusion.1 = bf16[2048,256]{1,0:T(8,128)(2,1)S(1)} fusion(bf16[2048,1152]{1,0:T(8,128)(2,1)} %bitcast.127, bf16[1152,128]{1,0:T(8,128)(2,1)S(1)} %copy-done.3, bf16[1152,128]{1,0:T(8,128)(2,1)S(1)} %copy-done.4), kind=kOutput, calls=%fused_computation.41 | convolution fusion | flops 1209663488 | bytes 6356992 | tf_op jit(solution)/shard_map/dot_general | solution.py:95
  192.4 4.3 %all-to-all-done = bf16[3,256,2048]{1,0,2:T(4,128)(2,1)} async-done(((bf16[3,256,2048]{1,0,2:T(4,128)(2,1)}), bf16[3,256,2048]{1,0,2:T(4,128)(2,1)}, u32[]{:S(2)}, u32[]{:S(2)}) %all-to-all-start) | async-done | bytes 3145760 | tf_op jit(solution)/shard_map/all_to_all | solution.py:67
  196.7 2.6 copy.45
  205.5 72.8 %while.11 = (s32[]{:T(128)}, bf16[8,512,1,128]{3,1,2,0:T(8,128)(2,1)}, bf16[8,512,1,128]{3,1,2,0:T(8,128)(2,1)S(1)}, bf16[4096,1,128]{2,0,1:T(8,128)(2,1)S(1)}, ...) while((s32[]{:T(128)}, ...), condition=%wide.region_7.8_spmd.clone, body=%wide.region_2.7_spmd.clone.sunk | while | flops 1642199040 | bytes 46035600 | solution.py:117
  208.4 2.5 fusion.73
  217.5 2.5 fusion.73
  226.6 2.5 fusion.73
  235.7 2.5 fusion.73
  253.9 2.5 fusion.73
  263.0 2.5 fusion.73
  272.1 2.5 fusion.73
  278.3 22.4 %all_to_all.43 = bf16[16,256,128]{2,1,0:T(8,128)(2,1)S(1)} all-to-all(bf16[16,256,128]{2,1,0:T(8,128)(2,1)} %bitcast.24), channel_id=1, replica_groups=mesh['req'=8,'sp'=16] {'sp'}, dimensions={0} | all-to-all | bytes 2097152 | tf_op jit(solution)/shard_map/all_to_all | solution.py:119
  (108 shorter events, 76.4 us)
Async XLA Ops:
  6.5 91.3 %copy-start = (bf16[1,256,3072]{2,1,0:T(8,128)(2,1)S(1)}, bf16[1,256,3072]{2,1,0:T(8,128)(2,1)}, u32[]{:S(2)}) copy-start(bf16[1,256,3072]{2,1,0:T(8,128)(2,1)} %param.12) | copy-start | bytes 4718596
  6.5 37.2 %all-gather.6.cloned.1.call-start = ((), (), s32[]{:S(2)}) async-start(), calls=%async_computation.5 | async-start | bytes 4718592 | tf_op jit(solution)/shard_map/all_gather | solution.py:46
  7.3 79.1 %all-gather.4.cloned.1.call-start = ((), (), s32[]{:S(2)}) async-start(), calls=%async_computation.4 | async-start | bytes 7077888 | tf_op jit(solution)/shard_map/all_gather | solution.py:45
  8.0 178.1 %all-gather.8.cloned.1.call-start = ((), (), s32[]{:S(2)}) async-start(), calls=%async_computation.6 | async-start | bytes 5013504 | tf_op jit(solution)/shard_map/all_gather | solution.py:93
  24.1 87.5 %all-to-all-start.1 = ((bf16[8,1,2]{2,1,0:T(2,128)(2,1)}), bf16[8,1,2]{2,1,0:T(2,128)(2,1)S(1)}, u32[]{:S(2)}, u32[]{:S(2)}) async-start(bf16[8,1,2]{2,1,0:T(2,128)(2,1)} %copy.52), calls=%async_computation.1 | async-start | bytes 8192 | tf_op jit(solution)/shard_map/all_to_all | solution.py:86
  111.6 74.5 %copy-start.3 = (bf16[1152,128]{1,0:T(8,128)(2,1)S(1)}, bf16[1152,128]{1,0:T(8,128)(2,1)}, u32[]{:S(2)}) copy-start(bf16[1152,128]{1,0:T(8,128)(2,1)} %param.17) | copy-start | bytes 884740
  111.6 74.5 %copy-start.4 = (bf16[1152,128]{1,0:T(8,128)(2,1)S(1)}, bf16[1152,128]{1,0:T(8,128)(2,1)}, u32[]{:S(2)}) copy-start(bf16[1152,128]{1,0:T(8,128)(2,1)} %param.16) | copy-start | bytes 884740
  111.7 85.1 %all-to-all-start = ((bf16[3,256,2048]{1,0,2:T(4,128)(2,1)}), bf16[3,256,2048]{1,0,2:T(4,128)(2,1)}, u32[]{:S(2)}, u32[]{:S(2)}) async-start(bf16[3,256,2048]{1,0,2:T(4,128)(2,1)} %copy.44), calls=%async_computation | async-start | bytes 8388608 | tf_op jit(solution)/shard_map/all_to_all | solution.py:67
  206.9 1.5 copy-start.2
  216.0 1.5 copy-start.2
  225.1 1.5 copy-start.2
  234.2 1.5 copy-start.2
  243.3 1.5 copy-start.2
  252.3 1.5 copy-start.2
  261.4 1.5 copy-start.2
  270.5 1.5 copy-start.2
  278.3 26.0 %copy-start.1 = (bf16[1,256,3072]{2,1,0:T(8,128)(2,1)S(1)}, bf16[1,256,3072]{2,1,0:T(8,128)(2,1)}, u32[]{:S(2)}) copy-start(bf16[1,256,3072]{2,1,0:T(8,128)(2,1)} %param.12) | copy-start | bytes 4718596
Sparse Core Ops, SparseCore 0:
  9.1 34.6 all-gather.5
  45.4 40.8 all-gather.3
  88.5 97.5 all-gather.7
where the time goes:
time: 312 us; the launch traced here: 311 us
  waiting for transfers between devices  116 us (37%)
  matrix products  78.6 us (25%)
  blocking collectives  34.8 us (11%)
  local copies, waits for them, and re-layouts  30.9 us (10%)
  other arithmetic  25.6 us (8%)
  between operations  14 us (4%)
  starting transfers between devices  10.4 us (3%)
    all_gather x1, waiting for transfers between devices, shards(): piece = lax.all_gather(got_rows, 'sp', axis=1, tiled=True)  67.2 us
    dot_general x16, matrix products, softmax_apply(): jnp.einsum('hqk,khd->qhd', weights, value_rows, preferred_element_type=jn...  35 us
    all_gather x1, waiting for transfers between devices, shards(): lax.all_gather(lowfactor_reducing_matrix, 'req', axis=0, tiled=True)  34.2 us
    all_to_all x1, blocking collectives, shards(): lax.all_to_all(per_heads, 'sp', split_axis=0, concat_axis=1, tiled=True)  22.4 us
    reduce_sum x16, other arithmetic, softmax_apply(): jnp.sum(weights, axis=-1, keepdims=True)  19.6 us
    dot_general x16, matrix products, softmax_apply(): jnp.einsum('qhd,khd->hqk', query_block, key_rows, preferred_element_type=...  17.4 us
    all_to_all x1, blocking collectives, shards(): lax.all_to_all(slot_rows, 'req', split_axis=0, concat_axis=0, tiled=True)  12.3 us
    dot_general x1, matrix products, shards(): jnp.einsum('a,adr->dr', pick_adapter, bank_down, preferred_element_type=j...  10.7 us
  transfers between devices with their start and end apart: 5, of which 4 were waited for; matrix products, arithmetic and copies ran while one was open for 16% of the time, Pallas kernels for 0%

commit v1 on v0

v1 whole, which is shorter than its diff:
```python
import functools

import numpy as np

import jax
import jax.numpy as jnp
from jax import lax
from jax.experimental import pallas as pl
from jax.experimental.pallas import tpu as pltpu
from jax.sharding import PartitionSpec as P

HD = 128
CAP = 2
TOK = 256
HEADS = 16
GROUPS = 8
SLOTS = GROUPS * CAP
IMG_TOK = 128
ENC = 1152
RANK = 64
WIDTH = 3072
FLAG_ROWS = 16
IMG_SOURCES = 4
PACKED = 3 * TOK + 2 * RANK

adapter_alpha = 16.0
ip_scale = 1.0

SCALE2 = float(np.log2(np.e) / np.sqrt(HD))
LEAST_TOTAL, LARGEST_TOTAL = 2.0**-80, 2.0**96

bf16 = jnp.bfloat16
f32 = jnp.float32
NT = (((1,), (1,)), ((), ()))
TN = (((0,), (0,)), ((), ()))


SMEM = pl.BlockSpec(memory_space=pltpu.SMEM)


def adapter_at(here_ref, index_ref):
    return (here_ref[0] // 2 - index_ref[here_ref[0]] // 4 + 4) % 4


def params(mib):
    return pltpu.CompilerParams(vmem_limit_bytes=mib << 20)


def moving(nbytes):
    return pl.CostEstimate(flops=0, bytes_accessed=nbytes, transcendentals=0)


def pack_kernel(k_ref, v_ref, q_ref, o_ref):
    for h in range(HEADS):
        for p, x_ref in enumerate((k_ref, v_ref, q_ref)):
            o_ref[h, p * TOK : (p + 1) * TOK] = x_ref[0, :, h * HD : (h + 1) * HD]


def pack_heads(planes):
    def plane(p):
        return pl.BlockSpec((1, TOK, HEADS * HD), lambda i: (p, 0, 0))

    return pl.pallas_call(
        pack_kernel,
        grid=(1,),
        in_specs=[plane(1), plane(2), plane(0)],
        out_specs=pl.BlockSpec((HEADS, 3 * TOK, HD), lambda i: (0, 0, 0)),
        out_shape=jax.ShapeDtypeStruct((HEADS, PACKED, HD), bf16),
        compiler_params=params(24),
        cost_estimate=moving(6 << 20),
    )(planes, planes, planes)


def choose_kernel(here_ref, index_ref, own_ref, other_ref, *o_refs):
    y, core = here_ref[0] // 2, here_ref[0] % 2
    for k in range(4):
        local = index_ref[(y + k) % 4 * 2 + core] % 4

        @pl.when(local // 2 == core)
        def _():
            o_refs[k][...] = own_ref[local % 2]

        @pl.when(local // 2 != core)
        def _():
            o_refs[k][...] = other_ref[local % 2]


def choose_adapters(here, index, own, other):
    vmem = pl.BlockSpec(memory_space=pltpu.VMEM)
    one = jax.ShapeDtypeStruct(own.shape[1:], bf16)
    return pl.pallas_call(
        choose_kernel,
        in_specs=[SMEM, SMEM, vmem, vmem],
        out_specs=[vmem] * 4,
        out_shape=[one] * 4,
        compiler_params=params(24),
        cost_estimate=moving(own.size * 8),
    )(here, index, own, other)


def rank_kernel(here_ref, index_ref, rank_ref, hidden_ref, a0, a1, a2, a3, _, o_ref, acts_ref, sems):
    def emit(a_ref):
        acts = lax.dot_general(a_ref[...], hidden_ref[...], NT, preferred_element_type=f32)
        kept = lax.broadcasted_iota(jnp.int32, acts.shape, 0) < rank_ref[here_ref[0]]
        acts = jnp.where(kept, acts, 0.0).astype(bf16)
        acts_ref[:RANK] = acts[:, :HD]
        acts_ref[RANK:] = acts[:, HD:]

    chosen = adapter_at(here_ref, index_ref)
    for j, a_ref in enumerate((a0, a1, a2, a3)):
        pl.when(chosen == j)(functools.partial(emit, a_ref))
    copies = [
        pltpu.make_async_copy(acts_ref, o_ref.at[h, pl.ds(3 * TOK, 2 * RANK)], sems.at[h])
        for h in range(HEADS)
    ]
    for copy in copies:
        copy.start()
    for copy in copies:
        copy.wait()


def add_ranks(here, index, rank, hidden, adapters, packed):
    down = pl.BlockSpec((RANK, WIDTH), lambda i: (0, 0))
    hbm = pl.BlockSpec(memory_space=pl.ANY)
    return pl.pallas_call(
        rank_kernel,
        grid=(1,),
        in_specs=[SMEM, SMEM, SMEM, pl.BlockSpec((TOK, WIDTH), lambda i: (0, 0))] + [down] * 4 + [hbm],
        out_specs=hbm,
        out_shape=jax.ShapeDtypeStruct(packed.shape, bf16),
        scratch_shapes=[pltpu.VMEM((2 * RANK, HD), bf16), pltpu.SemaphoreType.DMA((HEADS,))],
        input_output_aliases={8: 0},
        compiler_params=params(32),
        cost_estimate=pl.CostEstimate(
            flops=2 * TOK * WIDTH * RANK, bytes_accessed=4 << 20, transcendentals=0
        ),
    )(here, index, rank, hidden, *adapters, packed)


def image_kernel(here_ref, owner_ref, f_ref, wk_ref, wv_ref, *refs):
    outs, kv = refs[:GROUPS], refs[GROUPS]
    step = pl.program_id(0)
    weights = jnp.concatenate([wk_ref[...], wv_ref[...]], axis=1)
    rows = f_ref[...].reshape(IMG_SOURCES * 64, ENC)
    rows = jnp.dot(rows, weights, preferred_element_type=f32).reshape(IMG_SOURCES, 8, 8, 2 * HD)
    per_step = IMG_SOURCES * 8
    for i in range(8):
        kv[i, pl.ds(pl.multiple_of(step * per_step, per_step), per_step)] = rows[:, i].reshape(
            per_step, 2 * HD
        )

    @pl.when(step == pl.num_programs(0) - 1)
    def _():
        y, core = here_ref[0] // 2, here_ref[0] % 2
        for t in range(GROUPS):
            target = (y + t // 2) % 4 * 2 + (core + t % 2) % 2
            seen, held = jnp.int32(0), [jnp.int32(-1), jnp.int32(-1)]
            for i in range(8):
                hit = owner_ref[i] == target
                held = [jnp.where(hit & (seen == c), i, held[c]) for c in range(CAP)]
                seen = seen + hit.astype(jnp.int32)
            for c in range(CAP):
                got = kv[jnp.maximum(held[c], 0)]
                outs[t][c * IMG_TOK : (c + 1) * IMG_TOK] = jnp.where(held[c] >= 0, got, 0.0).astype(bf16)
            row = lax.broadcasted_iota(jnp.int32, (FLAG_ROWS, 2 * HD), 0)
            both = jnp.where(row == 0, held[0], held[1])
            outs[t][CAP * IMG_TOK :] = jnp.where(both >= 0, 1.0, 0.0).astype(bf16)


def place_images(here, owners, gathered, wk, wv):
    rows = CAP * IMG_TOK + FLAG_ROWS
    whole = pl.BlockSpec((ENC, HD), lambda i: (0, 0))
    return pl.pallas_call(
        image_kernel,
        grid=(HEADS // IMG_SOURCES,),
        in_specs=[SMEM, SMEM, pl.BlockSpec((IMG_SOURCES, 64, ENC), lambda i: (i, 0, 0)), whole, whole],
        out_specs=[pl.BlockSpec((rows, 2 * HD), lambda i: (0, 0))] * GROUPS,
        out_shape=[jax.ShapeDtypeStruct((rows, 2 * HD), bf16)] * GROUPS,
        scratch_shapes=[pltpu.VMEM((8, IMG_TOK, 2 * HD), f32)],
        compiler_params=params(60),
        cost_estimate=pl.CostEstimate(
            flops=2 * 1024 * ENC * 2 * HD, bytes_accessed=5 << 20, transcendentals=0
        ),
    )(here, owners, gathered, wk, wv)


def unpack_kernel(x_ref, o_ref):
    for h in range(HEADS):
        o_ref[0, :, h * HD : (h + 1) * HD] = x_ref[h]


def unpack_heads(per_head):
    rows = 128
    return pl.pallas_call(
        unpack_kernel,
        grid=(TOK // rows,),
        in_specs=[pl.BlockSpec((HEADS, rows, HD), lambda i: (0, i, 0))],
        out_specs=pl.BlockSpec((1, rows, HEADS * HD), lambda i: (0, i, 0)),
        out_shape=jax.ShapeDtypeStruct((1, TOK, HEADS * HD), bf16),
        compiler_params=pltpu.CompilerParams(vmem_limit_bytes=24 << 20),
        cost_estimate=pl.CostEstimate(flops=0, bytes_accessed=TOK * HEADS * HD * 4, transcendentals=0),
    )(per_head)


def attend_kernel(here_ref, index_ref, rank_ref, q_ref, acts_ref, kv_ref, u0, u1, u2, u3, *refs, per_step, chunk):
    images, (o_ref, q_s) = refs[:GROUPS], refs[GROUPS:]
    rows = per_step * TOK
    keys = HEADS * TOK
    blocks = chunk // TOK
    pairs = chunk // (CAP * IMG_TOK)
    img_chunks = SLOTS * IMG_TOK // chunk

    def own_key(c):
        return kv_ref[pl.ds(c * blocks, blocks), :TOK].reshape(chunk, HD)

    def own_val(c):
        return kv_ref[pl.ds(c * blocks, blocks), TOK:].reshape(chunk, HD)

    def img_part(c, low):
        return jnp.concatenate(
            [images[c * pairs + i][: CAP * IMG_TOK, low : low + HD] for i in range(pairs)], axis=0
        )

    def flag(s):
        rows16 = images[s // CAP][CAP * IMG_TOK :, :HD].astype(f32)
        return rows16[s % CAP : s % CAP + 1, :1] > 0.5

    chosen = adapter_at(here_ref, index_ref)
    rank = jnp.full((1, HD), rank_ref[here_ref[0]].astype(f32))
    scale = adapter_alpha / rank
    for j, up_ref in enumerate((u0, u1, u2, u3)):

        @pl.when(chosen == j)
        def _():
            up = up_ref[...]
            for i in range(per_step):
                for half in range(2):
                    acts = acts_ref[i, half * RANK : (half + 1) * RANK]
                    update = lax.dot_general(acts, up, TN, preferred_element_type=f32)
                    base = q_ref[i, half * HD : (half + 1) * HD].astype(f32)
                    q_s[i * TOK + half * HD : i * TOK + (half + 1) * HD] = (
                        base + scale * update
                    ).astype(bf16)

    q = q_s[...]

    def scores(key):
        return lax.dot_general(key, q, NT, preferred_element_type=f32) * SCALE2

    def finish(acc, total):
        return acc / jnp.sum(total, axis=0, keepdims=True)

    zeros = (jnp.zeros((HD, rows), f32), jnp.zeros((8, rows), f32))

    acc, own_total = zeros
    for c in range(keys // chunk):
        p = jnp.exp2(scores(own_key(c)))
        own_total = own_total + p.reshape(chunk // 8, 8, rows).sum(0)
        acc = acc + lax.dot_general(own_val(c), p.astype(bf16), TN, preferred_element_type=f32)
    own_total = jnp.sum(own_total, axis=0, keepdims=True)
    out = acc / own_total
    acc, img_total = zeros
    slots = chunk // IMG_TOK
    for c in range(img_chunks):
        p = jnp.exp2(scores(img_part(c, 0)))
        per_slot = p.reshape(slots, IMG_TOK // 8, 8, rows).sum(1)
        for s in range(slots):
            img_total = img_total + jnp.where(flag(c * slots + s), per_slot[s], 0.0)
        acc = acc + lax.dot_general(img_part(c, HD), p.astype(bf16), TN, preferred_element_type=f32)
    img_total = jnp.sum(img_total, axis=0, keepdims=True)
    out = out + ip_scale * (acc / img_total)
    o_ref[...] = out.T.astype(bf16).reshape(per_step, TOK, HD)
    low = jnp.min(jnp.minimum(own_total, img_total))
    high = jnp.max(jnp.maximum(own_total, img_total))
    in_range = (low >= LEAST_TOTAL) & (high <= LARGEST_TOTAL)

    @pl.when(jnp.logical_not(in_range))
    def _():
        def own_max(c, top):
            return jnp.maximum(top, scores(own_key(c)).reshape(chunk // 8, 8, rows).max(0))

        top = lax.fori_loop(0, keys // chunk, own_max, jnp.full((8, rows), -1e30, f32))
        top = jnp.max(top, axis=0, keepdims=True)

        def own_sum(c, carry):
            acc, total = carry
            p = jnp.exp2(scores(own_key(c)) - top)
            total = total + p.reshape(chunk // 8, 8, rows).sum(0)
            acc = acc + lax.dot_general(own_val(c), p.astype(bf16), TN, preferred_element_type=f32)
            return acc, total

        out = finish(*lax.fori_loop(0, keys // chunk, own_sum, zeros))

        def slot_scores(s):
            part = images[s // CAP][(s % CAP) * IMG_TOK : (s % CAP + 1) * IMG_TOK, :HD]
            return jnp.where(flag(s), scores(part), -1e30)

        top = jnp.full((8, rows), -1e30, f32)
        for s in range(SLOTS):
            top = jnp.maximum(top, slot_scores(s).reshape(IMG_TOK // 8, 8, rows).max(0))
        top = jnp.max(top, axis=0, keepdims=True)
        acc, total = zeros
        for s in range(SLOTS):
            p = jnp.exp2(slot_scores(s) - top)
            total = total + p.reshape(IMG_TOK // 8, 8, rows).sum(0)
            part = images[s // CAP][(s % CAP) * IMG_TOK : (s % CAP + 1) * IMG_TOK, HD:]
            acc = acc + lax.dot_general(part, p.astype(bf16), TN, preferred_element_type=f32)
        out = out + ip_scale * finish(acc, total)
        o_ref[...] = out.T.astype(bf16).reshape(per_step, TOK, HD)


def attend(here, index, rank, heads, adapters, images):
    per_step, chunk = 4, 512
    pairs = HEADS * TOK * (HEADS * TOK + SLOTS * IMG_TOK)
    up = pl.BlockSpec((RANK, HD), lambda i: (0, WIDTH // HD))
    image = pl.BlockSpec((CAP * IMG_TOK + FLAG_ROWS, 2 * HD), lambda i: (0, 0))
    return pl.pallas_call(
        functools.partial(attend_kernel, per_step=per_step, chunk=chunk),
        grid=(HEADS // per_step,),
        in_specs=[
            SMEM,
            SMEM,
            SMEM,
            pl.BlockSpec((per_step, TOK, HD), lambda i: (i, 2, 0)),
            pl.BlockSpec((per_step, 2 * RANK, HD), lambda i: (i, 3 * TOK // (2 * RANK), 0)),
            pl.BlockSpec((HEADS, 2 * TOK, HD), lambda i: (0, 0, 0)),
        ]
        + [up] * 4
        + [image] * GROUPS,
        out_specs=pl.BlockSpec((per_step, TOK, HD), lambda i: (i, 0, 0)),
        out_shape=jax.ShapeDtypeStruct((HEADS, TOK, HD), bf16),
        scratch_shapes=[pltpu.VMEM((per_step * TOK, HD), bf16)],
        compiler_params=params(60),
        cost_estimate=pl.CostEstimate(flops=pairs * HD * 4, bytes_accessed=6 << 20, transcendentals=pairs),
    )(here, index, rank, heads, heads, heads, *adapters, *images)


def along_req(k, d):
    return [(y * 2 + c, (y + k) % 4 * 2 + (c + d) % 2) for y in range(4) for c in range(2)]


def exchange(x):
    return lax.all_to_all(x, "sp", split_axis=0, concat_axis=0, tiled=True)


def after(x, *others):
    return lax.optimization_barrier((x,) + others)[0]


def shards(
    hidden,
    latent_query_key_value,
    features,
    image_request,
    image_key_weight,
    image_value_weight,
    caller_lowfactor_index,
    request_rank,
    lowfactor_reducing_matrix,
    lowfactor_expanding_matrix,
):
    here = lax.axis_index("req").reshape(1)
    place = lax.axis_index("sp").reshape(1)
    index, rank = caller_lowfactor_index, request_rank
    planes = latent_query_key_value[0].transpose(1, 0, 2)

    own = jnp.concatenate(
        [
            lowfactor_reducing_matrix.transpose(0, 2, 1),
            lax.dynamic_slice_in_dim(lowfactor_expanding_matrix, place[0] * HD, HD, 2),
        ],
        axis=2,
    )
    other = lax.ppermute(own, "req", along_req(0, 1))

    own_rows = after(features.reshape(64, ENC), own)
    gathered = exchange(jnp.broadcast_to(own_rows[None], (HEADS, 64, ENC)))

    chosen = choose_adapters(here, index, own, other)
    adapters = [chosen[0]] + [lax.ppermute(chosen[k], "req", along_req(k, 0)) for k in (1, 2, 3)]

    packed = add_ranks(here, index, rank, hidden[0], adapters, pack_heads(planes))
    heads = exchange(after(packed, gathered))

    ways = [(k, d) for k in range(4) for d in range(2)]
    placed = place_images(here, image_request[:, 0], gathered, image_key_weight, image_value_weight)
    images = [placed[0]] + [
        lax.ppermute(p, "req", along_req(k, d)) for p, (k, d) in zip(placed[1:], ways[1:])
    ]

    per_heads = attend(here, index, rank, heads, adapters, images)
    return unpack_heads(exchange(per_heads))


def solution(mesh):
    placed = (
        P("req", "sp", None),
        P("req", "sp", None, None),
        P("req", "sp", None),
        P("req", None),
        P(None, "sp"),
        P(None, "sp"),
        P(),
        P(),
        P("req", None, None),
        P("req", None, None),
    )
    return jax.shard_map(
        shards, mesh=mesh, in_specs=placed, out_specs=P("req", "sp", None), check_vma=False
    )
```

time: 312 us -> 207 us (0.66)
  Pallas kernels: 0 us -> 89.9 us
  matrix products: 78.6 us -> 0 us
  waiting for transfers between devices: 116 us -> 60.2 us
  other arithmetic: 25.6 us -> 1.19 us
  local copies, waits for them, and re-layouts: 30.9 us -> 7.45 us
  starting transfers between devices: 10.4 us -> 28.9 us
  blocking collectives: 34.8 us -> 19.1 us
  between operations: 14 us -> 0.18 us
    all_gather x3 -> x0, waiting for transfers between devices: 111 us -> none  [the longest x1 67.2 us: shards(): piece = lax.all_gather(got_rows, 'sp', axis=1, tiled=True)]
    pallas_call x0 -> x6, Pallas kernels: none -> 89.9 us  [the longest x1 80.4 us: attend(): pl.pallas_call(functools.partial(attend_kernel, per_step=per_step, chunk=...]
    dot_general x37 -> x0, matrix products: 78.6 us -> none  [the longest x16 35 us: softmax_apply(): jnp.einsum('hqk,khd->qhd', weights, value_rows, preferred_element_type=jn...]
    all_to_all x2, waiting for transfers between devices: 4.33 us -> 35.8 us  [exchange(): return lax.all_to_all(x, 'sp', split_axis=0, concat_axis=0, tiled=True)]
    ppermute x0 -> x11, waiting for transfers between devices: none -> 24.4 us  [the longest x3 14.2 us: shards(): lax.ppermute(chosen[k], 'req', along_req(k, 0))]
    reduce_sum x18 -> x0, other arithmetic: 20.6 us -> none  [the longest x16 19.6 us: softmax_apply(): jnp.sum(weights, axis=-1, keepdims=True)]
    ppermute x0 -> x11, starting transfers between devices: none -> 16.2 us  [the longest x7 10.3 us: shards(): lax.ppermute(p, 'req', along_req(k, d))]
    all_to_all x2 -> x1, blocking collectives: 34.8 us -> 19.1 us  [exchange(): return lax.all_to_all(x, 'sp', split_axis=0, concat_axis=0, tiled=True)]
  transfers between devices with their start and end apart: 5 -> 13, of which waited for: 4 -> 9; matrix products, arithmetic and copies ran while one was open for 16% -> 0% of each run, Pallas kernels for 0% -> 4%
where the time goes in v1:
time: 207 us
  Pallas kernels  89.9 us (43%)
  waiting for transfers between devices  60.2 us (29%)
  starting transfers between devices  28.9 us (14%)
  blocking collectives  19.1 us (9%)
  local copies, waits for them, and re-layouts  7.45 us (4%)
    pallas_call x1, Pallas kernels, attend(): pl.pallas_call(functools.partial(attend_kernel, per_step=per_step, chunk=...  80.4 us
    all_to_all x2, waiting for transfers between devices, exchange(): return lax.all_to_all(x, 'sp', split_axis=0, concat_axis=0, tiled=True)  35.8 us
    all_to_all x1, blocking collectives, exchange(): return lax.all_to_all(x, 'sp', split_axis=0, concat_axis=0, tiled=True)  19.1 us
    ppermute x3, waiting for transfers between devices, shards(): lax.ppermute(chosen[k], 'req', along_req(k, 0))  14.2 us
    all_to_all x2, starting transfers between devices, exchange(): return lax.all_to_all(x, 'sp', split_axis=0, concat_axis=0, tiled=True)  12.6 us
    ppermute x7, starting transfers between devices, shards(): lax.ppermute(p, 'req', along_req(k, d))  10.3 us
    ppermute x7, waiting for transfers between devices, shards(): lax.ppermute(p, 'req', along_req(k, d))  7.86 us
    ppermute x3, starting transfers between devices, shards(): lax.ppermute(chosen[k], 'req', along_req(k, 0))  5.89 us
  transfers between devices with their start and end apart: 13, of which 9 were waited for; matrix products, arithmetic and copies ran while one was open for 0% of the time, Pallas kernels for 4%

profile of v1, /device:TPU:0, one launch (start us, length us, event | category | flops | bytes accessed | tf_op | source)
XLA Modules:
  0.0 206.9 jit_solution(14284124672845459998)
XLA Ops:
  2.3 2.6 %broadcast_in_dim.2 = bf16[16,64,1152]{2,1,0:T(8,128)(2,1)} broadcast(bf16[64,1152]{1,0:T(8,128)(2,1)} %bitcast.13), dimensions={1,2} | broadcast | bytes 2506752 | tf_op jit(solution)/shard_map/broadcast_in_dim | solution.py:377
  4.9 8.1 %all-to-all-start = ((bf16[16,64,1152]{2,1,0:T(8,128)(2,1)}), bf16[16,64,1152]{2,1,0:T(8,128)(2,1)}, u32[]{:S(2)}, u32[]{:S(2)}) async-start(bf16[16,64,1152]{2,1,0:T(8,128)(2,1)} %broadcast_in_dim.2), calls=%async_computation | async-start | bytes 4718592 | tf_op jit(solution)/shard_map/all_to_all | solution.py:343
  13.1 2.3 %collective-permute-done.other_ref = bf16[2,64,3200]{2,1,0:T(8,128)(2,1)S(1)} collective-permute-done((bf16[2,64,3200]{2,1,0:T(8,128)(2,1)S(1)}, bf16[2,64,3200]{2,1,0:T(8,128)(2,1)S(1)}, u32[]{:S(2)}, u32[]{:S(2)}) %collective-permute-start) | collective-permute-done | bytes 819232 | tf_op jit(solution)/shard_map/ppermute | solution.py:374
  16.2 1.6 collective-permute-start.1
  17.9 2.9 %collective-permute-start.2 = (bf16[64,3200]{1,0:T(8,128)(2,1)S(1)}, bf16[64,3200]{1,0:T(8,128)(2,1)S(1)}, u32[]{:S(2)}, u32[]{:S(2)}) collective-permute-start(bf16[64,3200]{1,0:T(8,128)(2,1)S(1)} %get-tuple-element.21), channel_id=1, source_target_pairs={{0,64},{16,80},{32,96},{48,112},{64,0},{80,16},{96,32},{112,48},{1... | collective-permute-start | bytes 1228808 | tf_op jit(solution)/shard_map/ppermute | solution.py:380
  20.8 1.3 collective-permute-start.3
  22.1 1.9 copy-done.2
  24.8 4.3 %collective-permute-done.1.a1.u1 = bf16[64,3200]{1,0:T(8,128)(2,1)S(1)} collective-permute-done((bf16[64,3200]{1,0:T(8,128)(2,1)S(1)}, bf16[64,3200]{1,0:T(8,128)(2,1)S(1)}, u32[]{:S(2)}, u32[]{:S(2)}) %collective-permute-start.1) | collective-permute-done | bytes 409632 | tf_op jit(solution)/shard_map/ppermute | solution.py:380
  29.1 10.0 %collective-permute-done.2.a2.u2 = bf16[64,3200]{1,0:T(8,128)(2,1)S(1)} collective-permute-done((bf16[64,3200]{1,0:T(8,128)(2,1)S(1)}, bf16[64,3200]{1,0:T(8,128)(2,1)S(1)}, u32[]{:S(2)}, u32[]{:S(2)}) %collective-permute-start.2) | collective-permute-done | bytes 409632 | tf_op jit(solution)/shard_map/ppermute | solution.py:380
  39.1 2.0 shard_map.102
  41.2 1.8 copy-done.1
  43.0 5.6 %all-to-all-done.f_ref = bf16[16,64,1152]{2,1,0:T(8,128)(2,1)} async-done(((bf16[16,64,1152]{2,1,0:T(8,128)(2,1)}), bf16[16,64,1152]{2,1,0:T(8,128)(2,1)}, u32[]{:S(2)}, u32[]{:S(2)}) %all-to-all-start) | async-done | bytes 2359328 | tf_op jit(solution)/shard_map/all_to_all | solution.py:343
  48.6 4.5 %all-to-all-start.1 = ((bf16[16,896,128]{2,1,0:T(8,128)(2,1)}), bf16[16,896,128]{2,1,0:T(8,128)(2,1)}, u32[]{:S(2)}, u32[]{:S(2)}) async-start(bf16[16,896,128]{2,1,0:T(8,128)(2,1)} %copy-done.1), calls=%async_computation.1 | async-start | bytes 7340032 | tf_op jit(solution)/shard_map/all_to_all | solution.py:343
  53.1 4.7 %shard_map.103 = (bf16[272,256]{1,0:T(8,128)(2,1)}, bf16[272,256]{1,0:T(8,128)(2,1)}, bf16[272,256]{1,0:T(8,128)(2,1)}, bf16[272,256]{1,0:T(8,128)(2,1)}, bf16[2...) custom-call(s32[1]{0:T(128)} %bitcast.here_ref, ...), custom_call_target="tpu_custom_call" | custom-call | flops 603979776 | bytes 5242880 | tf_op jit(solution)/shard_map/pallas_call | solution.py:173
  57.8 1.3 collective-permute-start.10
  59.1 1.8 collective-permute-start.4
  61.0 4.0 %collective-permute-start.7 = (bf16[272,256]{1,0:T(8,128)(2,1)}, bf16[272,256]{1,0:T(8,128)(2,1)S(1)}, u32[]{:S(2)}, u32[]{:S(2)}) collective-permute-start(bf16[272,256]{1,0:T(8,128)(2,1)} %get-tuple-element.29), channel_id=1, source_target_pairs={{0,64},{16,80},{32,96},{48,112},{64,0},{80,16},{96,32},{112,48},{1... | collective-permute-start | bytes 417800 | tf_op jit(solution)/shard_map/ppermute | solution.py:388
  65.0 1.7 collective-permute-start.8
  66.7 1.4 collective-permute-start.9
  70.0 3.0 %collective-permute-done.7.refs_4_ = bf16[272,256]{1,0:T(8,128)(2,1)S(1)} collective-permute-done((bf16[272,256]{1,0:T(8,128)(2,1)}, bf16[272,256]{1,0:T(8,128)(2,1)S(1)}, u32[]{:S(2)}, u32[]{:S(2)}) %collective-permute-start.7) | collective-permute-done | bytes 139296 | tf_op jit(solution)/shard_map/ppermute | solution.py:388
  73.0 2.9 %collective-permute-done.8.refs_5_ = bf16[272,256]{1,0:T(8,128)(2,1)S(1)} collective-permute-done((bf16[272,256]{1,0:T(8,128)(2,1)}, bf16[272,256]{1,0:T(8,128)(2,1)S(1)}, u32[]{:S(2)}, u32[]{:S(2)}) %collective-permute-start.8) | collective-permute-done | bytes 139296 | tf_op jit(solution)/shard_map/ppermute | solution.py:388
  76.0 30.2 %all-to-all-done.1.q_ref.acts_ref.kv_ref = bf16[16,896,128]{2,1,0:T(8,128)(2,1)} async-done(((bf16[16,896,128]{2,1,0:T(8,128)(2,1)}), bf16[16,896,128]{2,1,0:T(8,128)(2,1)}, u32[]{:S(2)}, u32[]{:S(2)}) %all-to-all-start.1) | async-done | bytes 3670048 | tf_op jit(solution)/shard_map/all_to_all | solution.py:343
  106.2 80.4 %shard_map.104 = bf16[16,256,128]{2,1,0:T(8,128)(2,1)} custom-call(s32[1]{0:T(128)} %bitcast.here_ref, s32[8]{0:T(128)} %index_ref.5, s32[8]{0:T(128)} %rank_ref.3, bf16[16,896,128]{2,1,0:T(8,128)(2,1)} %all-to-all-done.1.q_ref.acts_ref.kv_ref, bf16[16,896,128]{2,1,0:T(8,128)(2,1)} %all-to-all-done.1.q_ref.acts_ref.kv_ref, ...), custom_call_target="tpu_custom_call" | custom-call | flops 12884901888 | bytes 6291456 | tf_op jit(solution)/shard_map/pallas_call | solution.py:317
  186.6 19.1 %all_to_all.15.x_ref = bf16[16,256,128]{2,1,0:T(8,128)(2,1)S(1)} all-to-all(bf16[16,256,128]{2,1,0:T(8,128)(2,1)} %shard_map.104), channel_id=1, replica_groups=mesh['req'=8,'sp'=16] {'sp'}, dimensions={0} | all-to-all | bytes 2097152 | tf_op jit(solution)/shard_map/all_to_all | solution.py:343
  (46 shorter events, 7.0 us)
Async XLA Ops:
  4.9 43.7 %all-to-all-start = ((bf16[16,64,1152]{2,1,0:T(8,128)(2,1)}), bf16[16,64,1152]{2,1,0:T(8,128)(2,1)}, u32[]{:S(2)}, u32[]{:S(2)}) async-start(bf16[16,64,1152]{2,1,0:T(8,128)(2,1)} %broadcast_in_dim.2), calls=%async_computation | async-start | bytes 4718592 | tf_op jit(solution)/shard_map/all_to_all | solution.py:343
  13.0 2.4 %collective-permute-start = (bf16[2,64,3200]{2,1,0:T(8,128)(2,1)S(1)}, bf16[2,64,3200]{2,1,0:T(8,128)(2,1)S(1)}, u32[]{:S(2)}, u32[]{:S(2)}) collective-permute-start(bf16[2,64,3200]{2,1,0:T(8,128)(2,1)S(1)} %pad_maximum_fusion.own_ref), channel_id=1, source_target_pairs={{0,16},{16,0},{32,48},{48,32},{64,80},{80,64},{96,112},{112,96},{1... | collective-permute-start | bytes 2457608 | tf_op jit(solution)/shard_map/ppermute | solution.py:374
  16.2 22.8 %copy-start.4 = (bf16[64,3200]{1,0:T(8,128)(2,1)}, bf16[64,3200]{1,0:T(8,128)(2,1)S(1)}, u32[]{:S(2)}) copy-start(bf16[64,3200]{1,0:T(8,128)(2,1)S(1)} %get-tuple-element.19.a0.u0) | copy-start | bytes 1228804
  16.2 12.9 %collective-permute-start.1 = (bf16[64,3200]{1,0:T(8,128)(2,1)S(1)}, bf16[64,3200]{1,0:T(8,128)(2,1)S(1)}, u32[]{:S(2)}, u32[]{:S(2)}) collective-permute-start(bf16[64,3200]{1,0:T(8,128)(2,1)S(1)} %get-tuple-element.20), channel_id=1, source_target_pairs={{0,32},{16,48},{32,64},{48,80},{64,96},{80,112},{96,0},{112,16},{1... | collective-permute-start | bytes 1228808 | tf_op jit(solution)/shard_map/ppermute | solution.py:380
  17.9 21.2 %collective-permute-start.2 = (bf16[64,3200]{1,0:T(8,128)(2,1)S(1)}, bf16[64,3200]{1,0:T(8,128)(2,1)S(1)}, u32[]{:S(2)}, u32[]{:S(2)}) collective-permute-start(bf16[64,3200]{1,0:T(8,128)(2,1)S(1)} %get-tuple-element.21), channel_id=1, source_target_pairs={{0,64},{16,80},{32,96},{48,112},{64,0},{80,16},{96,32},{112,48},{1... | collective-permute-start | bytes 1228808 | tf_op jit(solution)/shard_map/ppermute | solution.py:380
  20.8 18.3 %collective-permute-start.3 = (bf16[64,3200]{1,0:T(8,128)(2,1)S(1)}, bf16[64,3200]{1,0:T(8,128)(2,1)S(1)}, u32[]{:S(2)}, u32[]{:S(2)}) collective-permute-start(bf16[64,3200]{1,0:T(8,128)(2,1)S(1)} %get-tuple-element.22), channel_id=1, source_target_pairs={{0,96},{16,112},{32,0},{48,16},{64,32},{80,48},{96,64},{112,80},{1... | collective-permute-start | bytes 1228808 | tf_op jit(solution)/shard_map/ppermute | solution.py:380
  24.0 15.0 %copy-start.3 = (bf16[1,256,3072]{2,1,0:T(8,128)(2,1)S(1)}, bf16[1,256,3072]{2,1,0:T(8,128)(2,1)}, u32[]{:S(2)}) copy-start(bf16[1,256,3072]{2,1,0:T(8,128)(2,1)} %param.10) | copy-start | bytes 4718596
  24.0 15.0 %copy-start.9 = (s32[8]{0:T(128)S(1)}, s32[8]{0:T(128)}, u32[]{:S(2)}) copy-start(s32[8]{0:T(128)} %rank_ref.3) | copy-start | bytes 100
  29.1 12.0 %copy-start.5 = (bf16[64,3200]{1,0:T(8,128)(2,1)}, bf16[64,3200]{1,0:T(8,128)(2,1)S(1)}, u32[]{:S(2)}) copy-start(bf16[64,3200]{1,0:T(8,128)(2,1)S(1)} %collective-permute-done.1.a1.u1) | copy-start | bytes 1228804
  48.6 57.5 %all-to-all-start.1 = ((bf16[16,896,128]{2,1,0:T(8,128)(2,1)}), bf16[16,896,128]{2,1,0:T(8,128)(2,1)}, u32[]{:S(2)}, u32[]{:S(2)}) async-start(bf16[16,896,128]{2,1,0:T(8,128)(2,1)} %copy-done.1), calls=%async_computation.1 | async-start | bytes 7340032 | tf_op jit(solution)/shard_map/all_to_all | solution.py:343
  57.8 7.2 %collective-permute-start.10 = (bf16[272,256]{1,0:T(8,128)(2,1)}, bf16[272,256]{1,0:T(8,128)(2,1)S(1)}, u32[]{:S(2)}, u32[]{:S(2)}) collective-permute-start(bf16[272,256]{1,0:T(8,128)(2,1)} %get-tuple-element.32), channel_id=1, source_target_pairs={{0,112},{16,96},{32,16},{48,0},{64,48},{80,32},{96,80},{112,64},{1... | collective-permute-start | bytes 417800 | tf_op jit(solution)/shard_map/ppermute | solution.py:388
  59.1 7.6 %collective-permute-start.4 = (bf16[272,256]{1,0:T(8,128)(2,1)}, bf16[272,256]{1,0:T(8,128)(2,1)S(1)}, u32[]{:S(2)}, u32[]{:S(2)}) collective-permute-start(bf16[272,256]{1,0:T(8,128)(2,1)} %get-tuple-element.26), channel_id=1, source_target_pairs={{0,16},{16,0},{32,48},{48,32},{64,80},{80,64},{96,112},{112,96},{1... | collective-permute-start | bytes 417800 | tf_op jit(solution)/shard_map/ppermute | solution.py:388
  61.0 8.0 %collective-permute-start.5 = (bf16[272,256]{1,0:T(8,128)(2,1)}, bf16[272,256]{1,0:T(8,128)(2,1)S(1)}, u32[]{:S(2)}, u32[]{:S(2)}) collective-permute-start(bf16[272,256]{1,0:T(8,128)(2,1)} %get-tuple-element.27), channel_id=1, source_target_pairs={{0,32},{16,48},{32,64},{48,80},{64,96},{80,112},{96,0},{112,16},{1... | collective-permute-start | bytes 417800 | tf_op jit(solution)/shard_map/ppermute | solution.py:388
  61.0 9.1 %collective-permute-start.6 = (bf16[272,256]{1,0:T(8,128)(2,1)}, bf16[272,256]{1,0:T(8,128)(2,1)S(1)}, u32[]{:S(2)}, u32[]{:S(2)}) collective-permute-start(bf16[272,256]{1,0:T(8,128)(2,1)} %get-tuple-element.28), channel_id=1, source_target_pairs={{0,48},{16,32},{32,80},{48,64},{64,112},{80,96},{96,16},{112,0},{1... | collective-permute-start | bytes 417800 | tf_op jit(solution)/shard_map/ppermute | solution.py:388
  61.0 12.1 %collective-permute-start.7 = (bf16[272,256]{1,0:T(8,128)(2,1)}, bf16[272,256]{1,0:T(8,128)(2,1)S(1)}, u32[]{:S(2)}, u32[]{:S(2)}) collective-permute-start(bf16[272,256]{1,0:T(8,128)(2,1)} %get-tuple-element.29), channel_id=1, source_target_pairs={{0,64},{16,80},{32,96},{48,112},{64,0},{80,16},{96,32},{112,48},{1... | collective-permute-start | bytes 417800 | tf_op jit(solution)/shard_map/ppermute | solution.py:388
  65.0 41.1 %copy-start.10 = (bf16[272,256]{1,0:T(8,128)(2,1)}, bf16[272,256]{1,0:T(8,128)(2,1)S(1)}, u32[]{:S(2)}) copy-start(bf16[272,256]{1,0:T(8,128)(2,1)S(1)} %collective-permute-done.10.refs_7_) | copy-start | bytes 417796
  65.0 11.0 %collective-permute-start.8 = (bf16[272,256]{1,0:T(8,128)(2,1)}, bf16[272,256]{1,0:T(8,128)(2,1)S(1)}, u32[]{:S(2)}, u32[]{:S(2)}) collective-permute-start(bf16[272,256]{1,0:T(8,128)(2,1)} %get-tuple-element.30), channel_id=1, source_target_pairs={{0,80},{16,64},{32,112},{48,96},{64,16},{80,0},{96,48},{112,32},{1... | collective-permute-start | bytes 417800 | tf_op jit(solution)/shard_map/ppermute | solution.py:388
  66.7 39.4 %copy-start.11 = (bf16[272,256]{1,0:T(8,128)(2,1)}, bf16[272,256]{1,0:T(8,128)(2,1)S(1)}, u32[]{:S(2)}) copy-start(bf16[272,256]{1,0:T(8,128)(2,1)S(1)} %collective-permute-done.4.refs_1_) | copy-start | bytes 417796
  66.7 9.3 %collective-permute-start.9 = (bf16[272,256]{1,0:T(8,128)(2,1)}, bf16[272,256]{1,0:T(8,128)(2,1)S(1)}, u32[]{:S(2)}, u32[]{:S(2)}) collective-permute-start(bf16[272,256]{1,0:T(8,128)(2,1)} %get-tuple-element.31), channel_id=1, source_target_pairs={{0,96},{16,112},{32,0},{48,16},{64,32},{80,48},{96,64},{112,80},{1... | collective-permute-start | bytes 417800 | tf_op jit(solution)/shard_map/ppermute | solution.py:388
  68.9 37.2 %copy-start.12 = (bf16[272,256]{1,0:T(8,128)(2,1)}, bf16[272,256]{1,0:T(8,128)(2,1)S(1)}, u32[]{:S(2)}) copy-start(bf16[272,256]{1,0:T(8,128)(2,1)S(1)} %collective-permute-done.5.refs_2_) | copy-start | bytes 417796
  70.0 36.1 %copy-start.13 = (bf16[272,256]{1,0:T(8,128)(2,1)}, bf16[272,256]{1,0:T(8,128)(2,1)S(1)}, u32[]{:S(2)}) copy-start(bf16[272,256]{1,0:T(8,128)(2,1)S(1)} %collective-permute-done.6.refs_3_) | copy-start | bytes 417796
  73.0 33.1 %copy-start.14 = (bf16[272,256]{1,0:T(8,128)(2,1)}, bf16[272,256]{1,0:T(8,128)(2,1)S(1)}, u32[]{:S(2)}) copy-start(bf16[272,256]{1,0:T(8,128)(2,1)S(1)} %collective-permute-done.7.refs_4_) | copy-start | bytes 417796
  76.0 30.2 %copy-start.15 = (bf16[272,256]{1,0:T(8,128)(2,1)}, bf16[272,256]{1,0:T(8,128)(2,1)S(1)}, u32[]{:S(2)}) copy-start(bf16[272,256]{1,0:T(8,128)(2,1)S(1)} %collective-permute-done.8.refs_5_) | copy-start | bytes 417796
  76.0 30.2 %copy-start.16 = (bf16[272,256]{1,0:T(8,128)(2,1)}, bf16[272,256]{1,0:T(8,128)(2,1)S(1)}, u32[]{:S(2)}) copy-start(bf16[272,256]{1,0:T(8,128)(2,1)S(1)} %collective-permute-done.9.refs_6_) | copy-start | bytes 417796
  (6 other events, 19.5 us)

commit v2 on v1

v2 whole, which is shorter than its diff:
```python
import functools

import numpy as np

import jax
import jax.numpy as jnp
from jax import lax
from jax.experimental import pallas as pl
from jax.experimental.pallas import tpu as pltpu
from jax.sharding import PartitionSpec as P

HD = 128
CAP = 2
TOK = 256
HEADS = 16
GROUPS = 8
SLOTS = GROUPS * CAP
IMG_TOK = 128
ENC = 1152
RANK = 64
WIDTH = 3072
FLAG_ROWS = 16
HALF = TOK // 2
PACKED = 2 * TOK + 2 * RANK

adapter_alpha = 16.0
ip_scale = 1.0

SCALE2 = float(np.log2(np.e) / np.sqrt(HD))
LEAST_TOTAL, LARGEST_TOTAL = 2.0**-80, 2.0**96

bf16 = jnp.bfloat16
f32 = jnp.float32
NT = (((1,), (1,)), ((), ()))
TN = (((0,), (0,)), ((), ()))


SMEM = pl.BlockSpec(memory_space=pltpu.SMEM)


def params(mib):
    return pltpu.CompilerParams(vmem_limit_bytes=mib << 20)


def moving(nbytes):
    return pl.CostEstimate(flops=0, bytes_accessed=nbytes, transcendentals=0)


def pack_first_kernel(k_ref, v_ref, q_ref, o_ref):
    for h in range(HEADS):
        o_ref[h, :HALF] = k_ref[0, :, h * HD : (h + 1) * HD]
        o_ref[h, HALF:TOK] = v_ref[0, :, h * HD : (h + 1) * HD]
        o_ref[h, TOK:] = q_ref[0, :, h * HD : (h + 1) * HD]


def pack_second_kernel(k_ref, v_ref, o_ref):
    for h in range(HEADS):
        o_ref[h, :HALF] = k_ref[0, :, h * HD : (h + 1) * HD]
        o_ref[h, HALF:] = v_ref[0, :, h * HD : (h + 1) * HD]


def half_of(plane, part):
    return pl.BlockSpec((1, HALF, HEADS * HD), lambda i: (plane, part, 0))


def pack_first(planes):
    return pl.pallas_call(
        pack_first_kernel,
        grid=(1,),
        in_specs=[half_of(1, 0), half_of(2, 0), pl.BlockSpec((1, TOK, HEADS * HD), lambda i: (0, 0, 0))],
        out_specs=pl.BlockSpec((HEADS, 2 * TOK, HD), lambda i: (0, 0, 0)),
        out_shape=jax.ShapeDtypeStruct((HEADS, PACKED, HD), bf16),
        compiler_params=params(24),
        cost_estimate=moving(4 << 20),
    )(planes, planes, planes)


def pack_second(planes):
    return pl.pallas_call(
        pack_second_kernel,
        grid=(1,),
        in_specs=[half_of(1, 1), half_of(2, 1)],
        out_specs=pl.BlockSpec((HEADS, TOK, HD), lambda i: (0, 0, 0)),
        out_shape=jax.ShapeDtypeStruct((HEADS, TOK, HD), bf16),
        compiler_params=params(24),
        cost_estimate=moving(2 << 20),
    )(planes, planes)


def choose_kernel(here_ref, index_ref, own_ref, other_ref, o_ref):
    core = here_ref[0] % 2
    for y in range(4):
        local = index_ref[y * 2 + core] % 4

        @pl.when(local // 2 == core)
        def _():
            o_ref[y] = own_ref[local % 2]

        @pl.when(local // 2 != core)
        def _():
            o_ref[y] = other_ref[local % 2]


def choose_adapters(here, index, own, other):
    vmem = pl.BlockSpec(memory_space=pltpu.VMEM)
    return pl.pallas_call(
        choose_kernel,
        in_specs=[SMEM, SMEM, vmem, vmem],
        out_specs=vmem,
        out_shape=jax.ShapeDtypeStruct((4,) + own.shape[1:], bf16),
        compiler_params=params(24),
        cost_estimate=moving(own.size * 8),
    )(here, index, own, other)


def holder(here, index):
    return index[here[0]] // 4


def rank_kernel(here_ref, index_ref, rank_ref, hidden_ref, a_ref, _, o_ref, acts_ref, sems):
    acts = lax.dot_general(hidden_ref[...], a_ref[0], NT, preferred_element_type=f32)
    kept = lax.broadcasted_iota(jnp.int32, acts.shape, 1) < rank_ref[here_ref[0]]
    acts = jnp.where(kept, acts, 0.0)
    acts_ref[...] = jnp.concatenate([acts[:HALF], acts[HALF:]], axis=1).astype(bf16)
    copies = [
        pltpu.make_async_copy(acts_ref, o_ref.at[h, pl.ds(2 * TOK, 2 * RANK)], sems.at[h])
        for h in range(HEADS)
    ]
    for copy in copies:
        copy.start()
    for copy in copies:
        copy.wait()


def add_ranks(here, index, rank, hidden, adapters, packed):
    hbm = pl.BlockSpec(memory_space=pl.ANY)
    return pl.pallas_call(
        rank_kernel,
        grid_spec=pltpu.PrefetchScalarGridSpec(
            num_scalar_prefetch=3,
            grid=(1,),
            in_specs=[
                pl.BlockSpec((TOK, WIDTH), lambda i, here, index, rank: (0, 0)),
                pl.BlockSpec((1, RANK, WIDTH), lambda i, here, index, rank: (holder(here, index), 0, 0)),
                hbm,
            ],
            out_specs=hbm,
            scratch_shapes=[pltpu.VMEM((HALF, 2 * RANK), bf16), pltpu.SemaphoreType.DMA((HEADS,))],
        ),
        out_shape=jax.ShapeDtypeStruct(packed.shape, bf16),
        input_output_aliases={5: 0},
        compiler_params=params(32),
        cost_estimate=pl.CostEstimate(
            flops=2 * TOK * WIDTH * RANK, bytes_accessed=4 << 20, transcendentals=0
        ),
    )(here, index, rank, hidden, adapters, packed)


def image_kernel(here_ref, owner_ref, wk_ref, wv_ref, *refs):
    pieces, outs, kv = refs[:8], refs[8 : 8 + GROUPS], refs[8 + GROUPS]
    weights = jnp.concatenate([wk_ref[...], wv_ref[...]], axis=1)
    for p, piece in enumerate(pieces):
        half, shift = p // 4, p % 4
        rows = jnp.dot(piece[...], weights, preferred_element_type=f32).reshape(4, 4, 8, 2 * HD)
        for i in range(4):
            kv[half * 4 + i, shift * 32 : (shift + 1) * 32] = rows[:, i].reshape(32, 2 * HD)
    y, core = here_ref[0] // 2, here_ref[0] % 2
    for t in range(GROUPS):
        target = (y + t // 2) % 4 * 2 + (core + t % 2) % 2
        seen, held = jnp.int32(0), [jnp.int32(-1), jnp.int32(-1)]
        for i in range(8):
            hit = owner_ref[i] == target
            held = [jnp.where(hit & (seen == c), i, held[c]) for c in range(CAP)]
            seen = seen + hit.astype(jnp.int32)
        for c in range(CAP):
            got = kv[jnp.maximum(held[c], 0)]
            outs[t][c * IMG_TOK : (c + 1) * IMG_TOK] = jnp.where(held[c] >= 0, got, 0.0).astype(bf16)
        row = lax.broadcasted_iota(jnp.int32, (FLAG_ROWS, 2 * HD), 0)
        both = jnp.where(row == 0, held[0], held[1])
        outs[t][CAP * IMG_TOK :] = jnp.where(both >= 0, 1.0, 0.0).astype(bf16)


def place_images(here, owners, pieces, wk, wv):
    rows = CAP * IMG_TOK + FLAG_ROWS
    whole = pl.BlockSpec((ENC, HD), lambda i: (0, 0))
    return pl.pallas_call(
        image_kernel,
        grid=(1,),
        in_specs=[SMEM, SMEM, whole, whole] + [pl.BlockSpec((IMG_TOK, ENC), lambda i: (0, 0))] * 8,
        out_specs=[pl.BlockSpec((rows, 2 * HD), lambda i: (0, 0))] * GROUPS,
        out_shape=[jax.ShapeDtypeStruct((rows, 2 * HD), bf16)] * GROUPS,
        scratch_shapes=[pltpu.VMEM((8, IMG_TOK, 2 * HD), f32)],
        compiler_params=params(60),
        cost_estimate=pl.CostEstimate(
            flops=2 * 1024 * ENC * 2 * HD, bytes_accessed=5 << 20, transcendentals=0
        ),
    )(here, owners, wk, wv, *pieces)


def unpack_kernel(x_ref, o_ref):
    for h in range(HEADS):
        o_ref[0, :, h * HD : (h + 1) * HD] = x_ref[h]


def unpack_heads(per_head):
    rows = 128
    return pl.pallas_call(
        unpack_kernel,
        grid=(TOK // rows,),
        in_specs=[pl.BlockSpec((HEADS, rows, HD), lambda i: (0, i, 0))],
        out_specs=pl.BlockSpec((1, rows, HEADS * HD), lambda i: (0, i, 0)),
        out_shape=jax.ShapeDtypeStruct((1, TOK, HEADS * HD), bf16),
        compiler_params=pltpu.CompilerParams(vmem_limit_bytes=24 << 20),
        cost_estimate=pl.CostEstimate(flops=0, bytes_accessed=TOK * HEADS * HD * 4, transcendentals=0),
    )(per_head)


def transposed_scores(key, q):
    return lax.dot_general(key, q, NT, preferred_element_type=f32) * SCALE2


def weigh(val, p):
    return lax.dot_general(val, p.astype(bf16), TN, preferred_element_type=f32)


def by_eights(x):
    return x.reshape(x.shape[0] // 8, 8, x.shape[1])


def in_range(total):
    return (jnp.min(total) >= LEAST_TOTAL) & (jnp.max(total) <= LARGEST_TOTAL)


def self_key(kv_ref, chunk, c):
    blocks = chunk // HALF
    return kv_ref[c * blocks : (c + 1) * blocks, :HALF].reshape(chunk, HD)


def self_val(kv_ref, chunk, c):
    blocks = chunk // HALF
    return kv_ref[c * blocks : (c + 1) * blocks, HALF:].reshape(chunk, HD)


def none_yet(rows):
    return jnp.zeros((HD, rows), f32), jnp.zeros((8, rows), f32)


def self_part(kv_ref, q, chunk):
    acc, total = none_yet(q.shape[0])
    for c in range(HEADS * HALF // chunk):
        p = jnp.exp2(transposed_scores(self_key(kv_ref, chunk, c), q))
        total = total + by_eights(p).sum(0)
        acc = acc + weigh(self_val(kv_ref, chunk, c), p)
    return acc, jnp.sum(total, axis=0, keepdims=True)


def self_part_by_maximum(kv_ref, q, chunk):
    chunks, top = HEADS * HALF // chunk, jnp.full((8, q.shape[0]), -1e30, f32)
    for c in range(chunks):
        top = jnp.maximum(top, by_eights(transposed_scores(self_key(kv_ref, chunk, c), q)).max(0))
    top = jnp.max(top, axis=0, keepdims=True)
    acc, total = none_yet(q.shape[0])
    for c in range(chunks):
        p = jnp.exp2(transposed_scores(self_key(kv_ref, chunk, c), q) - top)
        total = total + by_eights(p).sum(0)
        acc = acc + weigh(self_val(kv_ref, chunk, c), p)
    return acc, jnp.sum(total, axis=0, keepdims=True), top


def slot_held(images, s):
    rows16 = images[s // CAP][CAP * IMG_TOK :, :HD].astype(f32)
    return rows16[s % CAP : s % CAP + 1, :1] > 0.5


def image_part(images, q, chunk):
    pairs, slots = chunk // (CAP * IMG_TOK), chunk // IMG_TOK

    def part(c, low):
        return jnp.concatenate(
            [images[c * pairs + i][: CAP * IMG_TOK, low : low + HD] for i in range(pairs)], axis=0
        )

    acc, total = none_yet(q.shape[0])
    for c in range(SLOTS // slots):
        p = jnp.exp2(transposed_scores(part(c, 0), q))
        per_slot = p.reshape(slots, IMG_TOK // 8, 8, q.shape[0]).sum(1)
        for s in range(slots):
            total = total + jnp.where(slot_held(images, c * slots + s), per_slot[s], 0.0)
        acc = acc + weigh(part(c, HD), p)
    return acc, jnp.sum(total, axis=0, keepdims=True)


def image_part_by_maximum(images, q):
    def slot_part(s, low):
        first = s % CAP * IMG_TOK
        return images[s // CAP][first : first + IMG_TOK, low : low + HD]

    def slot_scores(s):
        return jnp.where(slot_held(images, s), transposed_scores(slot_part(s, 0), q), -1e30)

    top = jnp.full((8, q.shape[0]), -1e30, f32)
    for s in range(SLOTS):
        top = jnp.maximum(top, by_eights(slot_scores(s)).max(0))
    top = jnp.max(top, axis=0, keepdims=True)
    acc, total = none_yet(q.shape[0])
    for s in range(SLOTS):
        p = jnp.exp2(slot_scores(s) - top)
        total = total + by_eights(p).sum(0)
        acc = acc + weigh(slot_part(s, HD), p)
    return acc, jnp.sum(total, axis=0, keepdims=True)


def first_kernel(
    here_ref, index_ref, rank_ref, q_ref, acts_ref, kv_ref, up_ref, *refs, per_step, chunk
):
    images, (q_s, acc_ref, sums_ref, img_ref, up_s) = refs[:GROUPS], refs[GROUPS:]

    @pl.when(pl.program_id(0) == 0)
    def _():
        up = up_ref[0]
        none = jnp.zeros_like(up)
        up_s[:, :HD] = jnp.concatenate([up, none], axis=0)
        up_s[:, HD:] = jnp.concatenate([none, up], axis=0)

    rank = jnp.full((1, 2 * HD), rank_ref[here_ref[0]].astype(f32))
    acts = acts_ref[...].reshape(per_step * HALF, 2 * RANK)
    update = adapter_alpha / rank * jnp.dot(acts, up_s[...], preferred_element_type=f32)
    parts = [update[:, half * HD : (half + 1) * HD].reshape(per_step, HALF, HD) for half in range(2)]
    q = (q_ref[...].astype(f32) + jnp.concatenate(parts, axis=1)).astype(bf16)
    q_s[...] = q
    q = q.reshape(per_step * TOK, HD)

    acc, total = self_part(kv_ref, q, chunk)
    img_acc, img_total = image_part(images, q, chunk)
    acc_ref[0] = acc
    sums_ref[0, :8] = jnp.broadcast_to(total, (8, total.shape[1]))
    sums_ref[0, 8:] = jnp.zeros((8, total.shape[1]), f32)
    img_ref[0] = img_acc / img_total

    @pl.when(jnp.logical_not(in_range(total)))
    def _():
        acc, total, top = self_part_by_maximum(kv_ref, q_s[...].reshape(per_step * TOK, HD), chunk)
        acc_ref[0] = acc
        sums_ref[0, :8] = jnp.broadcast_to(total, (8, total.shape[1]))
        sums_ref[0, 8:] = jnp.broadcast_to(top, (8, total.shape[1]))

    @pl.when(jnp.logical_not(in_range(img_total)))
    def _():
        acc, total = image_part_by_maximum(images, q_s[...].reshape(per_step * TOK, HD))
        img_ref[0] = acc / total


def second_kernel(q_ref, kv_ref, acc_ref, sums_ref, img_ref, o_ref, *, per_step, chunk):
    q = q_ref[...].reshape(per_step * TOK, HD)

    def emit(acc, total, top):
        total1, top1 = sums_ref[0, :1], sums_ref[0, 8:9]
        both = jnp.maximum(top, top1)
        scale, scale1 = jnp.exp2(top - both), jnp.exp2(top1 - both)
        own = (acc * scale + acc_ref[0] * scale1) / (total * scale + total1 * scale1)
        out = own + ip_scale * img_ref[0]
        o_ref[...] = out.T.astype(bf16).reshape(per_step, TOK, HD)

    acc, total = self_part(kv_ref, q, chunk)
    emit(acc, total, jnp.zeros_like(total))

    @pl.when(jnp.logical_not(in_range(total)))
    def _():
        emit(*self_part_by_maximum(kv_ref, q_ref[...].reshape(per_step * TOK, HD), chunk))


PER_STEP, CHUNK = 4, 1024
STEPS = HEADS // PER_STEP
HEAD_BLOCK = pl.BlockSpec((PER_STEP, TOK, HD), lambda i: (i, 0, 0))
KEYS_BLOCK = pl.BlockSpec((HEADS, TOK, HD), lambda i: (0, 0, 0))
WIDE_BLOCK = pl.BlockSpec((1, HD, PER_STEP * TOK), lambda i: (i, 0, 0))
SUMS_BLOCK = pl.BlockSpec((1, 16, PER_STEP * TOK), lambda i: (i, 0, 0))


def attention_cost(keys):
    pairs = HEADS * TOK * keys
    return pl.CostEstimate(flops=pairs * HD * 4, bytes_accessed=8 << 20, transcendentals=pairs)


def attend_first(here, index, rank, first, adapters, images):
    def block(shape, at):
        return pl.BlockSpec(shape, lambda i, here, index, rank: at(i, here, index))

    each = lambda i, here, index: (i, 0, 0)
    image = block((CAP * IMG_TOK + FLAG_ROWS, 2 * HD), lambda i, here, index: (0, 0))
    wide = jax.ShapeDtypeStruct((STEPS, HD, PER_STEP * TOK), f32)
    return pl.pallas_call(
        functools.partial(first_kernel, per_step=PER_STEP, chunk=CHUNK),
        grid_spec=pltpu.PrefetchScalarGridSpec(
            num_scalar_prefetch=3,
            grid=(STEPS,),
            in_specs=[
                block((PER_STEP, TOK, HD), lambda i, here, index: (i, 1, 0)),
                block((PER_STEP, 2 * RANK, HD), lambda i, here, index: (i, 2 * TOK // (2 * RANK), 0)),
                block((HEADS, TOK, HD), lambda i, here, index: (0, 0, 0)),
                block((1, RANK, HD), lambda i, here, index: (holder(here, index), 0, WIDTH // HD)),
            ]
            + [image] * GROUPS,
            out_specs=[
                block((PER_STEP, TOK, HD), each),
                block((1, HD, PER_STEP * TOK), each),
                block((1, 16, PER_STEP * TOK), each),
                block((1, HD, PER_STEP * TOK), each),
            ],
            scratch_shapes=[pltpu.VMEM((2 * RANK, 2 * HD), bf16)],
        ),
        out_shape=[
            jax.ShapeDtypeStruct((HEADS, TOK, HD), bf16),
            wide,
            jax.ShapeDtypeStruct((STEPS, 16, PER_STEP * TOK), f32),
            wide,
        ],
        compiler_params=params(60),
        cost_estimate=attention_cost(HEADS * HALF + SLOTS * IMG_TOK),
    )(here, index, rank, first, first, first, adapters, *images)


def attend_second(updated, second, acc, sums, image):
    return pl.pallas_call(
        functools.partial(second_kernel, per_step=PER_STEP, chunk=CHUNK),
        grid=(STEPS,),
        in_specs=[HEAD_BLOCK, KEYS_BLOCK, WIDE_BLOCK, SUMS_BLOCK, WIDE_BLOCK],
        out_specs=HEAD_BLOCK,
        out_shape=jax.ShapeDtypeStruct((HEADS, TOK, HD), bf16),
        compiler_params=params(60),
        cost_estimate=attention_cost(HEADS * HALF),
    )(updated, second, acc, sums, image)


def along_x(k):
    return [(z * 4 + x, z * 4 + (x + k) % 4) for z in range(4) for x in range(4)]


def along_z(k):
    return [(z * 4 + x, ((z + k) % 4) * 4 + x) for z in range(4) for x in range(4)]


def along_req(k, d):
    return [(y * 2 + c, (y + k) % 4 * 2 + (c + d) % 2) for y in range(4) for c in range(2)]


def exchange(x):
    return lax.all_to_all(x, "sp", split_axis=0, concat_axis=0, tiled=True)


def after(x, *others):
    return lax.optimization_barrier((x,) + others)[0]


def shards(
    hidden,
    latent_query_key_value,
    features,
    image_request,
    image_key_weight,
    image_value_weight,
    caller_lowfactor_index,
    request_rank,
    lowfactor_reducing_matrix,
    lowfactor_expanding_matrix,
):
    here = lax.axis_index("req").reshape(1)
    place = lax.axis_index("sp").reshape(1)
    index, rank = caller_lowfactor_index, request_rank
    planes = latent_query_key_value[0].transpose(1, 0, 2)

    own = jnp.concatenate(
        [
            lowfactor_reducing_matrix.transpose(0, 2, 1),
            lax.dynamic_slice_in_dim(lowfactor_expanding_matrix, place[0] * HD, HD, 2),
        ],
        axis=2,
    )
    other = lax.ppermute(own, "req", along_req(0, 1))

    half = features.shape[0] // 2
    lines = []
    for part, way in ((features[:half], along_x), (features[half:], along_z)):
        line = [part] + [lax.ppermute(part, "sp", way(k)) for k in (1, 2, 3)]
        lines.append(jnp.stack(line).reshape(IMG_TOK, ENC))
    pieces = []
    for line, way in zip(lines, (along_z, along_x)):
        pieces += [line] + [lax.ppermute(line, "sp", way(k)) for k in (1, 2, 3)]

    chosen = choose_adapters(here, index, own, other)
    adapters = lax.all_to_all(
        chosen,
        "req",
        split_axis=0,
        concat_axis=0,
        tiled=True,
        axis_index_groups=[[y * 2 + core for y in range(4)] for core in range(2)],
    )

    packed = add_ranks(here, index, rank, hidden[0], adapters, pack_first(planes))
    first = exchange(after(packed, *pieces))

    ways = [(k, d) for k in range(4) for d in range(2)]
    placed = place_images(here, image_request[:, 0], pieces, image_key_weight, image_value_weight)
    images = [placed[0]] + [
        lax.ppermute(p, "req", along_req(k, d)) for p, (k, d) in zip(placed[1:], ways[1:])
    ]

    second = exchange(after(pack_second(planes), first, *images))
    updated, acc, sums, image = attend_first(here, index, rank, first, adapters, images)
    per_heads = attend_second(updated, second, acc, sums, image)
    return unpack_heads(exchange(per_heads))


def solution(mesh):
    placed = (
        P("req", "sp", None),
        P("req", "sp", None, None),
        P("req", "sp", None),
        P("req", None),
        P(None, "sp"),
        P(None, "sp"),
        P(),
        P(),
        P("req", None, None),
        P("req", None, None),
    )
    return jax.shard_map(
        shards, mesh=mesh, in_specs=placed, out_specs=P("req", "sp", None), check_vma=False
    )
```

time: 207 us -> 166 us (0.80)
  waiting for transfers between devices: 60.2 us -> 20.8 us
  Pallas kernels: 89.9 us -> 68 us
  starting transfers between devices: 28.9 us -> 46 us
    all_to_all x2, waiting for transfers between devices: 35.8 us -> 9.49 us  [exchange(): return lax.all_to_all(x, 'sp', split_axis=0, concat_axis=0, tiled=True)]
    pallas_call x4 -> x6, Pallas kernels: 88 us -> 64.9 us  [the longest x1 31.7 us: attend_first(): pl.pallas_call(functools.partial(first_kernel, per_step=PER_STEP, chunk=C...]
    ppermute x3 -> x12, starting transfers between devices: 5.89 us -> 21.9 us  [the longest x6 12.1 us: shards(): pieces += [line] + [lax.ppermute(line, 'sp', way(k)) for k in (1, 2, 3)]]
    ppermute x3 -> x12, waiting for transfers between devices: 14.2 us -> 2.95 us  [the longest x6 2.94 us: shards(): pieces += [line] + [lax.ppermute(line, 'sp', way(k)) for k in (1, 2, 3)]]
    all_to_all x0 -> x1, starting transfers between devices: none -> 4.68 us  [shards(): lax.all_to_all(chosen, 'req', split_axis=0, concat_axis=0, tiled=True, ax...]
    unnamed x34 -> x40, local copies, waits for them, and re-layouts: 4.81 us -> 9.47 us
    ppermute x7, starting transfers between devices: 10.3 us -> 6.94 us  [shards(): lax.ppermute(p, 'req', along_req(k, d))]
    broadcast_in_dim x1 -> x0, local copies, waits for them, and re-layouts: 2.64 us -> none  [shards(): gathered = exchange(jnp.broadcast_to(own_rows[None], (HEADS, 64, ENC)))]
  transfers between devices with their start and end apart: 13 -> 23, of which waited for: 9 -> 6; matrix products, arithmetic and copies ran while one was open for 0% -> 0% of each run, Pallas kernels for 4% -> 24%
where the time goes in v2:
time: 166 us
  Pallas kernels  68 us (41%)
  starting transfers between devices  46 us (28%)
  waiting for transfers between devices  20.8 us (13%)
  blocking collectives  19.9 us (12%)
  local copies, waits for them, and re-layouts  9.5 us (6%)
    pallas_call x1, Pallas kernels, attend_first(): pl.pallas_call(functools.partial(first_kernel, per_step=PER_STEP, chunk=C...  31.7 us
    pallas_call x1, Pallas kernels, attend_second(): pl.pallas_call(functools.partial(second_kernel, per_step=PER_STEP, chunk=...  24.3 us
    all_to_all x1, blocking collectives, exchange(): return lax.all_to_all(x, 'sp', split_axis=0, concat_axis=0, tiled=True)  19.9 us
    all_to_all x2, starting transfers between devices, exchange(): return lax.all_to_all(x, 'sp', split_axis=0, concat_axis=0, tiled=True)  12.4 us
    ppermute x6, starting transfers between devices, shards(): pieces += [line] + [lax.ppermute(line, 'sp', way(k)) for k in (1, 2, 3)]  12.1 us
    ppermute x6, starting transfers between devices, shards(): line = [part] + [lax.ppermute(part, 'sp', way(k)) for k in (1, 2, 3)]  9.81 us
    all_to_all x2, waiting for transfers between devices, exchange(): return lax.all_to_all(x, 'sp', split_axis=0, concat_axis=0, tiled=True)  9.49 us
    unnamed x40, local copies, waits for them, and re-layouts  9.47 us
  transfers between devices with their start and end apart: 23, of which 6 were waited for; matrix products, arithmetic and copies ran while one was open for 0% of the time, Pallas kernels for 24%

profile of v2, /device:TPU:0, one launch (start us, length us, event | category | flops | bytes accessed | tf_op | source)
XLA Modules:
  0.0 165.7 jit_solution(12931018692269611143)
XLA Ops:
  2.4 2.3 %collective-permute-done.other_ref = bf16[2,64,3200]{2,1,0:T(8,128)(2,1)S(1)} collective-permute-done((bf16[2,64,3200]{2,1,0:T(8,128)(2,1)S(1)}, bf16[2,64,3200]{2,1,0:T(8,128)(2,1)S(1)}, u32[]{:S(2)}, u32[]{:S(2)}) %collective-permute-start) | collective-permute-done | bytes 819232 | tf_op jit(solution)/shard_map/ppermute | solution.py:479
  5.3 1.9 %shard_map.100 = bf16[4,64,3200]{2,1,0:T(8,128)(2,1)} custom-call(s32[1]{0:T(128)} %bitcast.here_ref, s32[8]{0:T(128)S(1)} %copy-done.5, bf16[2,64,3200]{2,1,0:T(8,128)(2,1)S(1)} %pad_maximum_fusion.own_ref, bf16[2,64,3200]{2,1,0:T(8,128)(2,1)S(1)} %collective-permute-done.other_ref), custom_call_target="tpu_custom_call" | custom-call | bytes 3276800 | tf_op jit(solution)/shard_map/pallas_call | solution.py:106
  7.3 4.7 %all-to-all-start = ((bf16[4,64,3200]{2,1,0:T(8,128)(2,1)}), bf16[4,64,3200]{2,1,0:T(8,128)(2,1)S(1)}, u32[]{:S(2)}, u32[]{:S(2)}) async-start(bf16[4,64,3200]{2,1,0:T(8,128)(2,1)} %shard_map.100), calls=%async_computation | async-start | bytes 3276800 | tf_op jit(solution)/shard_map/all_to_all | solution.py:491
  12.0 2.8 %collective-permute-start.3 = (bf16[4,8,1152]{2,1,0:T(8,128)(2,1)S(1)}, bf16[4,8,1152]{2,1,0:T(8,128)(2,1)S(1)}, u32[]{:S(2)}, u32[]{:S(2)}) collective-permute-start(bf16[4,8,1152]{2,1,0:T(8,128)(2,1)S(1)} %get-tuple-element.36), channel_id=1, source_target_pairs={{0,3},{1,0},{2,1},{3,2},{4,7},{5,4},{6,5},{7,6},{8,11},{9,8},{10,9... | collective-permute-start | bytes 221192 | tf_op jit(solution)/shard_map/ppermute | solution.py:484
  16.5 4.0 %collective-permute-start.9 = (bf16[4,8,1152]{2,1,0:T(8,128)(2,1)S(1)}, bf16[4,8,1152]{2,1,0:T(8,128)(2,1)S(1)}, u32[]{:S(2)}, u32[]{:S(2)}) collective-permute-start(bf16[4,8,1152]{2,1,0:T(8,128)(2,1)S(1)} %get-tuple-element.35), channel_id=1, source_target_pairs={{0,12},{1,13},{2,14},{3,15},{4,0},{5,1},{6,2},{7,3},{8,4},{9,5},{1... | collective-permute-start | bytes 221192 | tf_op jit(solution)/shard_map/ppermute | solution.py:484
  21.9 2.3 %collective-permute-start.4 = (bf16[128,1152]{1,0:T(8,128)(2,1)S(1)}, bf16[128,1152]{1,0:T(8,128)(2,1)S(1)}, u32[]{:S(2)}, u32[]{:S(2)}) collective-permute-start(bf16[128,1152]{1,0:T(8,128)(2,1)S(1)} %bitcast.25), channel_id=1, source_target_pairs={{0,4},{1,5},{2,6},{3,7},{4,8},{5,9},{6,10},{7,11},{8,12},{9,13},{1... | collective-permute-start | bytes 884744 | tf_op jit(solution)/shard_map/ppermute | solution.py:488
  24.1 3.1 %collective-permute-start.5 = (bf16[128,1152]{1,0:T(8,128)(2,1)S(1)}, bf16[128,1152]{1,0:T(8,128)(2,1)S(1)}, u32[]{:S(2)}, u32[]{:S(2)}) collective-permute-start(bf16[128,1152]{1,0:T(8,128)(2,1)S(1)} %bitcast.26), channel_id=1, source_target_pairs={{0,8},{1,9},{2,10},{3,11},{4,12},{5,13},{6,14},{7,15},{8,0},{9,1},... | collective-permute-start | bytes 884744 | tf_op jit(solution)/shard_map/ppermute | solution.py:488
  29.7 2.0 %collective-permute-start.11 = (bf16[128,1152]{1,0:T(8,128)(2,1)S(1)}, bf16[128,1152]{1,0:T(8,128)(2,1)}, u32[]{:S(2)}, u32[]{:S(2)}) collective-permute-start(bf16[128,1152]{1,0:T(8,128)(2,1)S(1)} %bitcast.30), channel_id=1, source_target_pairs={{0,2},{1,3},{2,0},{3,1},{4,6},{5,7},{6,4},{7,5},{8,10},{9,11},{10,... | collective-permute-start | bytes 884744 | tf_op jit(solution)/shard_map/ppermute | solution.py:488
  31.7 2.9 %collective-permute-done.4.refs_1_ = bf16[128,1152]{1,0:T(8,128)(2,1)S(1)} collective-permute-done((bf16[128,1152]{1,0:T(8,128)(2,1)S(1)}, bf16[128,1152]{1,0:T(8,128)(2,1)S(1)}, u32[]{:S(2)}, u32[]{:S(2)}) %collective-permute-start.4) | collective-permute-done | bytes 294944 | tf_op jit(solution)/shard_map/ppermute | solution.py:488
  34.6 2.3 %collective-permute-start.12 = (bf16[128,1152]{1,0:T(8,128)(2,1)S(1)}, bf16[128,1152]{1,0:T(8,128)(2,1)}, u32[]{:S(2)}, u32[]{:S(2)}) collective-permute-start(bf16[128,1152]{1,0:T(8,128)(2,1)S(1)} %bitcast.31), channel_id=1, source_target_pairs={{0,3},{1,0},{2,1},{3,2},{4,7},{5,4},{6,5},{7,6},{8,11},{9,8},{10,9... | collective-permute-start | bytes 884744 | tf_op jit(solution)/shard_map/ppermute | solution.py:488
  36.9 1.9 %copy-done.1 = bf16[1,256,3,2048]{3,1,2,0:T(8,128)(2,1)S(1)} copy-done((bf16[1,256,3,2048]{3,1,2,0:T(8,128)(2,1)S(1)}, bf16[1,256,3,2048]{3,1,2,0:T(8,128)(2,1)}, u32[]{:S(2)}) %copy-start.1) | copy-done | bytes 3145752
  40.6 2.0 %copy-done.4 = bf16[1,256,3072]{2,1,0:T(8,128)(2,1)S(1)} copy-done((bf16[1,256,3072]{2,1,0:T(8,128)(2,1)S(1)}, bf16[1,256,3072]{2,1,0:T(8,128)(2,1)}, u32[]{:S(2)}) %copy-start.4) | copy-done | bytes 1572888
  42.6 2.1 %shard_map.102 = bf16[16,640,128]{2,1,0:T(8,128)(2,1)} custom-call(s32[1]{0:T(128)} %bitcast.here_ref, s32[8]{0:T(128)S(1)} %copy-done.6, s32[8]{0:T(128)S(1)} %copy-done.7, bf16[256,3072]{1,0:T(8,128)(2,1)S(1)} %bitcast.24, bf16[4,64,3200]{2,1,0:T(8,128)(2,1)S(1)} %all-to-all-done.a_ref.up_ref, ...), custom_call_target="tpu_custom_call", output_to_operand_aliasing={{}: (5, {})} | custom-call | flops 100663296 | bytes 4194304 | tf_op jit(solution)/shard_map/pallas_call | solution.py:137
  45.5 7.9 %all-to-all-start.1 = ((bf16[16,640,128]{2,1,0:T(8,128)(2,1)}), bf16[16,640,128]{2,1,0:T(8,128)(2,1)S(1)}, u32[]{:S(2)}, u32[]{:S(2)}) async-start(bf16[16,640,128]{2,1,0:T(8,128)(2,1)} %shard_map.102), calls=%async_computation.1 | async-start | bytes 5242880 | tf_op jit(solution)/shard_map/all_to_all | solution.py:448
  53.4 3.8 %shard_map.103 = (bf16[272,256]{1,0:T(8,128)(2,1)}, bf16[272,256]{1,0:T(8,128)(2,1)}, bf16[272,256]{1,0:T(8,128)(2,1)}, bf16[272,256]{1,0:T(8,128)(2,1)}, bf16[2...) custom-call(s32[1]{0:T(128)} %bitcast.here_ref, ...), custom_call_target="tpu_custom_call" | custom-call | flops 603979776 | bytes 5242880 | tf_op jit(solution)/shard_map/pallas_call | solution.py:186
  59.1 2.7 %collective-permute-start.16 = (bf16[272,256]{1,0:T(8,128)(2,1)}, bf16[272,256]{1,0:T(8,128)(2,1)S(1)}, u32[]{:S(2)}, u32[]{:S(2)}) collective-permute-start(bf16[272,256]{1,0:T(8,128)(2,1)} %get-tuple-element.24), channel_id=1, source_target_pairs={{0,64},{16,80},{32,96},{48,112},{64,0},{80,16},{96,32},{112,48},{1... | collective-permute-start | bytes 417800 | tf_op jit(solution)/shard_map/ppermute | solution.py:506
  65.3 1.9 %copy-done.2 = bf16[1,256,3,2048]{3,1,2,0:T(8,128)(2,1)S(1)} copy-done((bf16[1,256,3,2048]{3,1,2,0:T(8,128)(2,1)S(1)}, bf16[1,256,3,2048]{3,1,2,0:T(8,128)(2,1)}, u32[]{:S(2)}) %copy-start.2) | copy-done | bytes 3145752
  68.3 2.8 %collective-permute-done.16.refs_4_ = bf16[272,256]{1,0:T(8,128)(2,1)S(1)} collective-permute-done((bf16[272,256]{1,0:T(8,128)(2,1)}, bf16[272,256]{1,0:T(8,128)(2,1)S(1)}, u32[]{:S(2)}, u32[]{:S(2)}) %collective-permute-start.16) | collective-permute-done | bytes 139296 | tf_op jit(solution)/shard_map/ppermute | solution.py:506
  71.1 2.0 %collective-permute-done.17.refs_5_ = bf16[272,256]{1,0:T(8,128)(2,1)S(1)} collective-permute-done((bf16[272,256]{1,0:T(8,128)(2,1)}, bf16[272,256]{1,0:T(8,128)(2,1)S(1)}, u32[]{:S(2)}, u32[]{:S(2)}) %collective-permute-start.17) | collective-permute-done | bytes 139296 | tf_op jit(solution)/shard_map/ppermute | solution.py:506
  74.5 9.5 %all-to-all-done.1.q_ref.acts_ref.kv_ref = bf16[16,640,128]{2,1,0:T(8,128)(2,1)S(1)} async-done(((bf16[16,640,128]{2,1,0:T(8,128)(2,1)}), bf16[16,640,128]{2,1,0:T(8,128)(2,1)S(1)}, u32[]{:S(2)}, u32[]{:S(2)}) %all-to-all-start.1) | async-done | bytes 2621472 | tf_op jit(solution)/shard_map/all_to_all | solution.py:448
  84.0 4.5 %all-to-all-start.2 = ((bf16[16,256,128]{2,1,0:T(8,128)(2,1)}), bf16[16,256,128]{2,1,0:T(8,128)(2,1)}, u32[]{:S(2)}, u32[]{:S(2)}) async-start(bf16[16,256,128]{2,1,0:T(8,128)(2,1)} %shard_map.105), calls=%async_computation.2 | async-start | bytes 2097152 | tf_op jit(solution)/shard_map/all_to_all | solution.py:448
  88.5 31.7 %shard_map.104 = (bf16[16,256,128]{2,1,0:T(8,128)(2,1)}, f32[4,128,1024]{2,1,0:T(8,128)}, f32[4,16,1024]{2,1,0:T(8,128)}, f32[4,128,1024]{2,1,0:T(8,128)}) custom-call(s32[1]{0:T(128)} %bitcast.here_ref, s32[8]{0:T(128)} %index_ref.5, s32[8]{0:T(128)} %rank_ref.3, bf16[16,640,128]{2,1,0:T(8,128)(2,1)} %copy-done.8, bf16[16,640,128]{2,1,0:T(8,128)(2,1)} %copy-done.8, ...), custom_call_target="tpu_custom_call" | custom-call | flops 8589934592 | bytes 8388608 | tf_op jit(solution)/shard_map/pallas_call | solution.py:392
  120.3 24.3 %shard_map.106 = bf16[16,256,128]{2,1,0:T(8,128)(2,1)} custom-call(bf16[16,256,128]{2,1,0:T(8,128)(2,1)} %get-tuple-element.28.q_ref, bf16[16,256,128]{2,1,0:T(8,128)(2,1)} %all-to-all-done.2.kv_ref, f32[4,128,1024]{2,1,0:T(8,128)} %get-tuple-element.30.acc_ref, f32[4,16,1024]{2,1,0:T(8,128)} %get-tuple-element.31.sums_ref, ...), custom_call_target="tpu_custom_call" | custom-call | flops 4294967296 | bytes 8388608 | tf_op jit(solution)/shard_map/pallas_call | solution.py:424
  144.6 19.9 %all_to_all.20.x_ref = bf16[16,256,128]{2,1,0:T(8,128)(2,1)S(1)} all-to-all(bf16[16,256,128]{2,1,0:T(8,128)(2,1)} %shard_map.106), channel_id=1, replica_groups=mesh['req'=8,'sp'=16] {'sp'}, dimensions={0} | all-to-all | bytes 2097152 | tf_op jit(solution)/shard_map/all_to_all | solution.py:448
  (76 shorter events, 19.9 us)
Async XLA Ops:
  2.3 2.4 %collective-permute-start = (bf16[2,64,3200]{2,1,0:T(8,128)(2,1)S(1)}, bf16[2,64,3200]{2,1,0:T(8,128)(2,1)S(1)}, u32[]{:S(2)}, u32[]{:S(2)}) collective-permute-start(bf16[2,64,3200]{2,1,0:T(8,128)(2,1)S(1)} %pad_maximum_fusion.own_ref), channel_id=1, source_target_pairs={{0,16},{16,0},{32,48},{48,32},{64,80},{80,64},{96,112},{112,96},{1... | collective-permute-start | bytes 2457608 | tf_op jit(solution)/shard_map/ppermute | solution.py:479
  7.3 33.3 %all-to-all-start = ((bf16[4,64,3200]{2,1,0:T(8,128)(2,1)}), bf16[4,64,3200]{2,1,0:T(8,128)(2,1)S(1)}, u32[]{:S(2)}, u32[]{:S(2)}) async-start(bf16[4,64,3200]{2,1,0:T(8,128)(2,1)} %shard_map.100), calls=%async_computation | async-start | bytes 3276800 | tf_op jit(solution)/shard_map/all_to_all | solution.py:491
  12.0 8.6 %collective-permute-start.3 = (bf16[4,8,1152]{2,1,0:T(8,128)(2,1)S(1)}, bf16[4,8,1152]{2,1,0:T(8,128)(2,1)S(1)}, u32[]{:S(2)}, u32[]{:S(2)}) collective-permute-start(bf16[4,8,1152]{2,1,0:T(8,128)(2,1)S(1)} %get-tuple-element.36), channel_id=1, source_target_pairs={{0,3},{1,0},{2,1},{3,2},{4,7},{5,4},{6,5},{7,6},{8,11},{9,8},{10,9... | collective-permute-start | bytes 221192 | tf_op jit(solution)/shard_map/ppermute | solution.py:484
  14.8 7.0 %collective-permute-start.2 = (bf16[4,8,1152]{2,1,0:T(8,128)(2,1)S(1)}, bf16[4,8,1152]{2,1,0:T(8,128)(2,1)S(1)}, u32[]{:S(2)}, u32[]{:S(2)}) collective-permute-start(bf16[4,8,1152]{2,1,0:T(8,128)(2,1)S(1)} %get-tuple-element.36), channel_id=1, source_target_pairs={{0,2},{1,3},{2,0},{3,1},{4,6},{5,7},{6,4},{7,5},{8,10},{9,11},{10,... | collective-permute-start | bytes 221192 | tf_op jit(solution)/shard_map/ppermute | solution.py:484
  15.6 6.2 %collective-permute-start.1 = (bf16[4,8,1152]{2,1,0:T(8,128)(2,1)S(1)}, bf16[4,8,1152]{2,1,0:T(8,128)(2,1)S(1)}, u32[]{:S(2)}, u32[]{:S(2)}) collective-permute-start(bf16[4,8,1152]{2,1,0:T(8,128)(2,1)S(1)} %get-tuple-element.36), channel_id=1, source_target_pairs={{0,1},{1,2},{2,3},{3,0},{4,5},{5,6},{6,7},{7,4},{8,9},{9,10},{10,1... | collective-permute-start | bytes 221192 | tf_op jit(solution)/shard_map/ppermute | solution.py:484
  16.5 10.8 %collective-permute-start.9 = (bf16[4,8,1152]{2,1,0:T(8,128)(2,1)S(1)}, bf16[4,8,1152]{2,1,0:T(8,128)(2,1)S(1)}, u32[]{:S(2)}, u32[]{:S(2)}) collective-permute-start(bf16[4,8,1152]{2,1,0:T(8,128)(2,1)S(1)} %get-tuple-element.35), channel_id=1, source_target_pairs={{0,12},{1,13},{2,14},{3,15},{4,0},{5,1},{6,2},{7,3},{8,4},{9,5},{1... | collective-permute-start | bytes 221192 | tf_op jit(solution)/shard_map/ppermute | solution.py:484
  20.5 7.8 %collective-permute-start.8 = (bf16[4,8,1152]{2,1,0:T(8,128)(2,1)S(1)}, bf16[4,8,1152]{2,1,0:T(8,128)(2,1)S(1)}, u32[]{:S(2)}, u32[]{:S(2)}) collective-permute-start(bf16[4,8,1152]{2,1,0:T(8,128)(2,1)S(1)} %get-tuple-element.35), channel_id=1, source_target_pairs={{0,8},{1,9},{2,10},{3,11},{4,12},{5,13},{6,14},{7,15},{8,0},{9,1},... | collective-permute-start | bytes 221192 | tf_op jit(solution)/shard_map/ppermute | solution.py:484
  20.5 7.8 %collective-permute-start.7 = (bf16[4,8,1152]{2,1,0:T(8,128)(2,1)S(1)}, bf16[4,8,1152]{2,1,0:T(8,128)(2,1)S(1)}, u32[]{:S(2)}, u32[]{:S(2)}) collective-permute-start(bf16[4,8,1152]{2,1,0:T(8,128)(2,1)S(1)} %get-tuple-element.35), channel_id=1, source_target_pairs={{0,4},{1,5},{2,6},{3,7},{4,8},{5,9},{6,10},{7,11},{8,12},{9,13},{1... | collective-permute-start | bytes 221192 | tf_op jit(solution)/shard_map/ppermute | solution.py:484
  21.8 18.7 %copy-start.9 = (bf16[4,4,8,1152]{3,2,1,0:T(8,128)(2,1)}, bf16[4,4,8,1152]{3,2,1,0:T(8,128)(2,1)S(1)}, u32[]{:S(2)}) copy-start(bf16[4,4,8,1152]{3,2,1,0:T(8,128)(2,1)S(1)} %pad_maximum_fusion.1) | copy-start | bytes 884740
  21.9 12.7 %collective-permute-start.4 = (bf16[128,1152]{1,0:T(8,128)(2,1)S(1)}, bf16[128,1152]{1,0:T(8,128)(2,1)S(1)}, u32[]{:S(2)}, u32[]{:S(2)}) collective-permute-start(bf16[128,1152]{1,0:T(8,128)(2,1)S(1)} %bitcast.25), channel_id=1, source_target_pairs={{0,4},{1,5},{2,6},{3,7},{4,8},{5,9},{6,10},{7,11},{8,12},{9,13},{1... | collective-permute-start | bytes 884744 | tf_op jit(solution)/shard_map/ppermute | solution.py:488
  24.1 20.6 %collective-permute-start.5 = (bf16[128,1152]{1,0:T(8,128)(2,1)S(1)}, bf16[128,1152]{1,0:T(8,128)(2,1)S(1)}, u32[]{:S(2)}, u32[]{:S(2)}) collective-permute-start(bf16[128,1152]{1,0:T(8,128)(2,1)S(1)} %bitcast.26), channel_id=1, source_target_pairs={{0,8},{1,9},{2,10},{3,11},{4,12},{5,13},{6,14},{7,15},{8,0},{9,1},... | collective-permute-start | bytes 884744 | tf_op jit(solution)/shard_map/ppermute | solution.py:488
  27.3 17.5 %collective-permute-start.6 = (bf16[128,1152]{1,0:T(8,128)(2,1)S(1)}, bf16[128,1152]{1,0:T(8,128)(2,1)}, u32[]{:S(2)}, u32[]{:S(2)}) collective-permute-start(bf16[128,1152]{1,0:T(8,128)(2,1)S(1)} %bitcast.27), channel_id=1, source_target_pairs={{0,12},{1,13},{2,14},{3,15},{4,0},{5,1},{6,2},{7,3},{8,4},{9,5},{1... | collective-permute-start | bytes 884744 | tf_op jit(solution)/shard_map/ppermute | solution.py:488
  28.3 16.4 %collective-permute-start.10 = (bf16[128,1152]{1,0:T(8,128)(2,1)S(1)}, bf16[128,1152]{1,0:T(8,128)(2,1)}, u32[]{:S(2)}, u32[]{:S(2)}) collective-permute-start(bf16[128,1152]{1,0:T(8,128)(2,1)S(1)} %bitcast.29), channel_id=1, source_target_pairs={{0,1},{1,2},{2,3},{3,0},{4,5},{5,6},{6,7},{7,4},{8,9},{9,10},{10,1... | collective-permute-start | bytes 884744 | tf_op jit(solution)/shard_map/ppermute | solution.py:488
  29.7 15.1 %collective-permute-start.11 = (bf16[128,1152]{1,0:T(8,128)(2,1)S(1)}, bf16[128,1152]{1,0:T(8,128)(2,1)}, u32[]{:S(2)}, u32[]{:S(2)}) collective-permute-start(bf16[128,1152]{1,0:T(8,128)(2,1)S(1)} %bitcast.30), channel_id=1, source_target_pairs={{0,2},{1,3},{2,0},{3,1},{4,6},{5,7},{6,4},{7,5},{8,10},{9,11},{10,... | collective-permute-start | bytes 884744 | tf_op jit(solution)/shard_map/ppermute | solution.py:488
  34.6 10.2 %collective-permute-start.12 = (bf16[128,1152]{1,0:T(8,128)(2,1)S(1)}, bf16[128,1152]{1,0:T(8,128)(2,1)}, u32[]{:S(2)}, u32[]{:S(2)}) collective-permute-start(bf16[128,1152]{1,0:T(8,128)(2,1)S(1)} %bitcast.31), channel_id=1, source_target_pairs={{0,3},{1,0},{2,1},{3,2},{4,7},{5,4},{6,5},{7,6},{8,11},{9,8},{10,9... | collective-permute-start | bytes 884744 | tf_op jit(solution)/shard_map/ppermute | solution.py:488
  45.5 38.5 %all-to-all-start.1 = ((bf16[16,640,128]{2,1,0:T(8,128)(2,1)}), bf16[16,640,128]{2,1,0:T(8,128)(2,1)S(1)}, u32[]{:S(2)}, u32[]{:S(2)}) async-start(bf16[16,640,128]{2,1,0:T(8,128)(2,1)} %shard_map.102), calls=%async_computation.1 | async-start | bytes 5242880 | tf_op jit(solution)/shard_map/all_to_all | solution.py:448
  57.2 5.1 %collective-permute-start.13 = (bf16[272,256]{1,0:T(8,128)(2,1)}, bf16[272,256]{1,0:T(8,128)(2,1)S(1)}, u32[]{:S(2)}, u32[]{:S(2)}) collective-permute-start(bf16[272,256]{1,0:T(8,128)(2,1)} %get-tuple-element.21), channel_id=1, source_target_pairs={{0,16},{16,0},{32,48},{48,32},{64,80},{80,64},{96,112},{112,96},{1... | collective-permute-start | bytes 417800 | tf_op jit(solution)/shard_map/ppermute | solution.py:506
  57.2 8.0 %collective-permute-start.14 = (bf16[272,256]{1,0:T(8,128)(2,1)}, bf16[272,256]{1,0:T(8,128)(2,1)S(1)}, u32[]{:S(2)}, u32[]{:S(2)}) collective-permute-start(bf16[272,256]{1,0:T(8,128)(2,1)} %get-tuple-element.22), channel_id=1, source_target_pairs={{0,32},{16,48},{32,64},{48,80},{64,96},{80,112},{96,0},{112,16},{1... | collective-permute-start | bytes 417800 | tf_op jit(solution)/shard_map/ppermute | solution.py:506
  57.8 10.5 %collective-permute-start.15 = (bf16[272,256]{1,0:T(8,128)(2,1)}, bf16[272,256]{1,0:T(8,128)(2,1)S(1)}, u32[]{:S(2)}, u32[]{:S(2)}) collective-permute-start(bf16[272,256]{1,0:T(8,128)(2,1)} %get-tuple-element.23), channel_id=1, source_target_pairs={{0,48},{16,32},{32,80},{48,64},{64,112},{80,96},{96,16},{112,0},{1... | collective-permute-start | bytes 417800 | tf_op jit(solution)/shard_map/ppermute | solution.py:506
  59.1 12.1 %collective-permute-start.16 = (bf16[272,256]{1,0:T(8,128)(2,1)}, bf16[272,256]{1,0:T(8,128)(2,1)S(1)}, u32[]{:S(2)}, u32[]{:S(2)}) collective-permute-start(bf16[272,256]{1,0:T(8,128)(2,1)} %get-tuple-element.24), channel_id=1, source_target_pairs={{0,64},{16,80},{32,96},{48,112},{64,0},{80,16},{96,32},{112,48},{1... | collective-permute-start | bytes 417800 | tf_op jit(solution)/shard_map/ppermute | solution.py:506
  61.7 11.5 %collective-permute-start.17 = (bf16[272,256]{1,0:T(8,128)(2,1)}, bf16[272,256]{1,0:T(8,128)(2,1)S(1)}, u32[]{:S(2)}, u32[]{:S(2)}) collective-permute-start(bf16[272,256]{1,0:T(8,128)(2,1)} %get-tuple-element.25), channel_id=1, source_target_pairs={{0,80},{16,64},{32,112},{48,96},{64,16},{80,0},{96,48},{112,32},{1... | collective-permute-start | bytes 417800 | tf_op jit(solution)/shard_map/ppermute | solution.py:506
  62.3 10.9 %collective-permute-start.18 = (bf16[272,256]{1,0:T(8,128)(2,1)}, bf16[272,256]{1,0:T(8,128)(2,1)S(1)}, u32[]{:S(2)}, u32[]{:S(2)}) collective-permute-start(bf16[272,256]{1,0:T(8,128)(2,1)} %get-tuple-element.26), channel_id=1, source_target_pairs={{0,96},{16,112},{32,0},{48,16},{64,32},{80,48},{96,64},{112,80},{1... | collective-permute-start | bytes 417800 | tf_op jit(solution)/shard_map/ppermute | solution.py:506
  65.2 9.3 %collective-permute-start.19 = (bf16[272,256]{1,0:T(8,128)(2,1)}, bf16[272,256]{1,0:T(8,128)(2,1)}, u32[]{:S(2)}, u32[]{:S(2)}) collective-permute-start(bf16[272,256]{1,0:T(8,128)(2,1)} %get-tuple-element.27), channel_id=1, source_target_pairs={{0,112},{16,96},{32,16},{48,0},{64,48},{80,32},{96,80},{112,64},{1... | collective-permute-start | bytes 417800 | tf_op jit(solution)/shard_map/ppermute | solution.py:506
  84.0 36.3 %all-to-all-start.2 = ((bf16[16,256,128]{2,1,0:T(8,128)(2,1)}), bf16[16,256,128]{2,1,0:T(8,128)(2,1)}, u32[]{:S(2)}, u32[]{:S(2)}) async-start(bf16[16,256,128]{2,1,0:T(8,128)(2,1)} %shard_map.105), calls=%async_computation.2 | async-start | bytes 2097152 | tf_op jit(solution)/shard_map/all_to_all | solution.py:448
  (19 other events, 60.7 us)

commit v3 on v2

--- a/solution.py
+++ b/solution.py
@@ -87,26 +87,30 @@
     )(planes, planes)
 
 
-def choose_kernel(here_ref, index_ref, own_ref, other_ref, o_ref):
+def choose_kernel(here_ref, index_ref, own_ref, other_ref, o_ref, sems):
     core = here_ref[0] % 2
     for y in range(4):
         local = index_ref[y * 2 + core] % 4
 
         @pl.when(local // 2 == core)
         def _():
-            o_ref[y] = own_ref[local % 2]
+            pltpu.make_async_copy(own_ref.at[local % 2], o_ref.at[y], sems.at[y]).start()
 
         @pl.when(local // 2 != core)
         def _():
-            o_ref[y] = other_ref[local % 2]
+            pltpu.make_async_copy(other_ref.at[local % 2], o_ref.at[y], sems.at[y]).start()
+
+    for y in range(4):
+        pltpu.make_async_copy(own_ref.at[0], o_ref.at[y], sems.at[y]).wait()
 
 
 def choose_adapters(here, index, own, other):
-    vmem = pl.BlockSpec(memory_space=pltpu.VMEM)
+    hbm = pl.BlockSpec(memory_space=pl.ANY)
     return pl.pallas_call(
         choose_kernel,
-        in_specs=[SMEM, SMEM, vmem, vmem],
-        out_specs=vmem,
+        in_specs=[SMEM, SMEM, hbm, hbm],
+        out_specs=hbm,
+        scratch_shapes=[pltpu.SemaphoreType.DMA((4,))],
         out_shape=jax.ShapeDtypeStruct((4,) + own.shape[1:], bf16),
         compiler_params=params(24),
         cost_estimate=moving(own.size * 8),
@@ -359,7 +363,7 @@
         scale, scale1 = jnp.exp2(top - both), jnp.exp2(top1 - both)
         own = (acc * scale + acc_ref[0] * scale1) / (total * scale + total1 * scale1)
         out = own + ip_scale * img_ref[0]
-        o_ref[...] = out.T.astype(bf16).reshape(per_step, TOK, HD)
+        o_ref[...] = out.astype(bf16).T.reshape(per_step, TOK, HD)
 
     acc, total = self_part(kv_ref, q, chunk)
     emit(acc, total, jnp.zeros_like(total))

time: 166 us -> 166 us (level)
  transfers between devices with their start and end apart: 23 -> 23, of which waited for: 6 -> 6; matrix products, arithmetic and copies ran while one was open for 0% -> 0% of each run, Pallas kernels for 24% -> 25%
where the time goes in v3:
time: 166 us; the launch traced here: 165 us
  Pallas kernels  67.6 us (41%)
  starting transfers between devices  46 us (28%)
  waiting for transfers between devices  20.8 us (13%)
  blocking collectives  19.9 us (12%)
  local copies, waits for them, and re-layouts  9.51 us (6%)
    pallas_call x1, Pallas kernels, attend_first(): pl.pallas_call(functools.partial(first_kernel, per_step=PER_STEP, chunk=C...  31.7 us
    pallas_call x1, Pallas kernels, attend_second(): pl.pallas_call(functools.partial(second_kernel, per_step=PER_STEP, chunk=...  24.1 us
    all_to_all x1, blocking collectives, exchange(): return lax.all_to_all(x, 'sp', split_axis=0, concat_axis=0, tiled=True)  19.9 us
    all_to_all x2, starting transfers between devices, exchange(): return lax.all_to_all(x, 'sp', split_axis=0, concat_axis=0, tiled=True)  12.4 us
    ppermute x6, starting transfers between devices, shards(): pieces += [line] + [lax.ppermute(line, 'sp', way(k)) for k in (1, 2, 3)]  12.1 us
    ppermute x6, starting transfers between devices, shards(): line = [part] + [lax.ppermute(part, 'sp', way(k)) for k in (1, 2, 3)]  9.81 us
    all_to_all x2, waiting for transfers between devices, exchange(): return lax.all_to_all(x, 'sp', split_axis=0, concat_axis=0, tiled=True)  9.49 us
    unnamed x40, local copies, waits for them, and re-layouts  9.47 us
  transfers between devices with their start and end apart: 23, of which 6 were waited for; matrix products, arithmetic and copies ran while one was open for 0% of the time, Pallas kernels for 25%

profile of v3, /device:TPU:0, one launch (start us, length us, event | category | flops | bytes accessed | tf_op | source)
XLA Modules:
  0.0 165.4 jit_solution(220681918909509181)
XLA Ops:
  2.4 2.3 %collective-permute-done.other_ref = bf16[2,64,3200]{2,1,0:T(8,128)(2,1)S(1)} collective-permute-done((bf16[2,64,3200]{2,1,0:T(8,128)(2,1)S(1)}, bf16[2,64,3200]{2,1,0:T(8,128)(2,1)S(1)}, u32[]{:S(2)}, u32[]{:S(2)}) %collective-permute-start) | collective-permute-done | bytes 819232 | tf_op jit(solution)/shard_map/ppermute | solution.py:483
  5.3 1.8 %shard_map.100 = bf16[4,64,3200]{2,1,0:T(8,128)(2,1)} custom-call(s32[1]{0:T(128)} %bitcast.here_ref, s32[8]{0:T(128)S(1)} %copy-done.5, bf16[2,64,3200]{2,1,0:T(8,128)(2,1)S(1)} %pad_maximum_fusion.own_ref, bf16[2,64,3200]{2,1,0:T(8,128)(2,1)S(1)} %collective-permute-done.other_ref), custom_call_target="tpu_custom_call" | custom-call | bytes 3276800 | tf_op jit(solution)/shard_map/pallas_call | solution.py:109
  7.1 4.7 %all-to-all-start = ((bf16[4,64,3200]{2,1,0:T(8,128)(2,1)}), bf16[4,64,3200]{2,1,0:T(8,128)(2,1)S(1)}, u32[]{:S(2)}, u32[]{:S(2)}) async-start(bf16[4,64,3200]{2,1,0:T(8,128)(2,1)} %shard_map.100), calls=%async_computation | async-start | bytes 3276800 | tf_op jit(solution)/shard_map/all_to_all | solution.py:495
  11.8 2.8 %collective-permute-start.3 = (bf16[4,8,1152]{2,1,0:T(8,128)(2,1)S(1)}, bf16[4,8,1152]{2,1,0:T(8,128)(2,1)S(1)}, u32[]{:S(2)}, u32[]{:S(2)}) collective-permute-start(bf16[4,8,1152]{2,1,0:T(8,128)(2,1)S(1)} %get-tuple-element.36), channel_id=1, source_target_pairs={{0,3},{1,0},{2,1},{3,2},{4,7},{5,4},{6,5},{7,6},{8,11},{9,8},{10,9... | collective-permute-start | bytes 221192 | tf_op jit(solution)/shard_map/ppermute | solution.py:488
  16.4 4.0 %collective-permute-start.9 = (bf16[4,8,1152]{2,1,0:T(8,128)(2,1)S(1)}, bf16[4,8,1152]{2,1,0:T(8,128)(2,1)S(1)}, u32[]{:S(2)}, u32[]{:S(2)}) collective-permute-start(bf16[4,8,1152]{2,1,0:T(8,128)(2,1)S(1)} %get-tuple-element.35), channel_id=1, source_target_pairs={{0,12},{1,13},{2,14},{3,15},{4,0},{5,1},{6,2},{7,3},{8,4},{9,5},{1... | collective-permute-start | bytes 221192 | tf_op jit(solution)/shard_map/ppermute | solution.py:488
  21.7 2.3 %collective-permute-start.4 = (bf16[128,1152]{1,0:T(8,128)(2,1)S(1)}, bf16[128,1152]{1,0:T(8,128)(2,1)S(1)}, u32[]{:S(2)}, u32[]{:S(2)}) collective-permute-start(bf16[128,1152]{1,0:T(8,128)(2,1)S(1)} %bitcast.25), channel_id=1, source_target_pairs={{0,4},{1,5},{2,6},{3,7},{4,8},{5,9},{6,10},{7,11},{8,12},{9,13},{1... | collective-permute-start | bytes 884744 | tf_op jit(solution)/shard_map/ppermute | solution.py:492
  24.0 3.1 %collective-permute-start.5 = (bf16[128,1152]{1,0:T(8,128)(2,1)S(1)}, bf16[128,1152]{1,0:T(8,128)(2,1)S(1)}, u32[]{:S(2)}, u32[]{:S(2)}) collective-permute-start(bf16[128,1152]{1,0:T(8,128)(2,1)S(1)} %bitcast.26), channel_id=1, source_target_pairs={{0,8},{1,9},{2,10},{3,11},{4,12},{5,13},{6,14},{7,15},{8,0},{9,1},... | collective-permute-start | bytes 884744 | tf_op jit(solution)/shard_map/ppermute | solution.py:492
  29.5 2.0 %collective-permute-start.11 = (bf16[128,1152]{1,0:T(8,128)(2,1)S(1)}, bf16[128,1152]{1,0:T(8,128)(2,1)}, u32[]{:S(2)}, u32[]{:S(2)}) collective-permute-start(bf16[128,1152]{1,0:T(8,128)(2,1)S(1)} %bitcast.30), channel_id=1, source_target_pairs={{0,2},{1,3},{2,0},{3,1},{4,6},{5,7},{6,4},{7,5},{8,10},{9,11},{10,... | collective-permute-start | bytes 884744 | tf_op jit(solution)/shard_map/ppermute | solution.py:492
  31.5 2.9 %collective-permute-done.4.refs_1_ = bf16[128,1152]{1,0:T(8,128)(2,1)S(1)} collective-permute-done((bf16[128,1152]{1,0:T(8,128)(2,1)S(1)}, bf16[128,1152]{1,0:T(8,128)(2,1)S(1)}, u32[]{:S(2)}, u32[]{:S(2)}) %collective-permute-start.4) | collective-permute-done | bytes 294944 | tf_op jit(solution)/shard_map/ppermute | solution.py:492
  34.5 2.3 %collective-permute-start.12 = (bf16[128,1152]{1,0:T(8,128)(2,1)S(1)}, bf16[128,1152]{1,0:T(8,128)(2,1)}, u32[]{:S(2)}, u32[]{:S(2)}) collective-permute-start(bf16[128,1152]{1,0:T(8,128)(2,1)S(1)} %bitcast.31), channel_id=1, source_target_pairs={{0,3},{1,0},{2,1},{3,2},{4,7},{5,4},{6,5},{7,6},{8,11},{9,8},{10,9... | collective-permute-start | bytes 884744 | tf_op jit(solution)/shard_map/ppermute | solution.py:492
  36.8 1.9 %copy-done.1 = bf16[1,256,3,2048]{3,1,2,0:T(8,128)(2,1)S(1)} copy-done((bf16[1,256,3,2048]{3,1,2,0:T(8,128)(2,1)S(1)}, bf16[1,256,3,2048]{3,1,2,0:T(8,128)(2,1)}, u32[]{:S(2)}) %copy-start.1) | copy-done | bytes 3145752
  40.5 2.0 %copy-done.4 = bf16[1,256,3072]{2,1,0:T(8,128)(2,1)S(1)} copy-done((bf16[1,256,3072]{2,1,0:T(8,128)(2,1)S(1)}, bf16[1,256,3072]{2,1,0:T(8,128)(2,1)}, u32[]{:S(2)}) %copy-start.4) | copy-done | bytes 1572888
  42.4 2.1 %shard_map.102 = bf16[16,640,128]{2,1,0:T(8,128)(2,1)} custom-call(s32[1]{0:T(128)} %bitcast.here_ref, s32[8]{0:T(128)S(1)} %copy-done.6, s32[8]{0:T(128)S(1)} %copy-done.7, bf16[256,3072]{1,0:T(8,128)(2,1)S(1)} %bitcast.24, bf16[4,64,3200]{2,1,0:T(8,128)(2,1)S(1)} %all-to-all-done.a_ref.up_ref, ...), custom_call_target="tpu_custom_call", output_to_operand_aliasing={{}: (5, {})} | custom-call | flops 100663296 | bytes 4194304 | tf_op jit(solution)/shard_map/pallas_call | solution.py:141
  45.3 7.9 %all-to-all-start.1 = ((bf16[16,640,128]{2,1,0:T(8,128)(2,1)}), bf16[16,640,128]{2,1,0:T(8,128)(2,1)S(1)}, u32[]{:S(2)}, u32[]{:S(2)}) async-start(bf16[16,640,128]{2,1,0:T(8,128)(2,1)} %shard_map.102), calls=%async_computation.1 | async-start | bytes 5242880 | tf_op jit(solution)/shard_map/all_to_all | solution.py:452
  53.2 3.8 %shard_map.103 = (bf16[272,256]{1,0:T(8,128)(2,1)}, bf16[272,256]{1,0:T(8,128)(2,1)}, bf16[272,256]{1,0:T(8,128)(2,1)}, bf16[272,256]{1,0:T(8,128)(2,1)}, bf16[2...) custom-call(s32[1]{0:T(128)} %bitcast.here_ref, ...), custom_call_target="tpu_custom_call" | custom-call | flops 603979776 | bytes 5242880 | tf_op jit(solution)/shard_map/pallas_call | solution.py:190
  58.9 2.7 %collective-permute-start.16 = (bf16[272,256]{1,0:T(8,128)(2,1)}, bf16[272,256]{1,0:T(8,128)(2,1)S(1)}, u32[]{:S(2)}, u32[]{:S(2)}) collective-permute-start(bf16[272,256]{1,0:T(8,128)(2,1)} %get-tuple-element.24), channel_id=1, source_target_pairs={{0,64},{16,80},{32,96},{48,112},{64,0},{80,16},{96,32},{112,48},{1... | collective-permute-start | bytes 417800 | tf_op jit(solution)/shard_map/ppermute | solution.py:510
  65.1 1.9 %copy-done.2 = bf16[1,256,3,2048]{3,1,2,0:T(8,128)(2,1)S(1)} copy-done((bf16[1,256,3,2048]{3,1,2,0:T(8,128)(2,1)S(1)}, bf16[1,256,3,2048]{3,1,2,0:T(8,128)(2,1)}, u32[]{:S(2)}) %copy-start.2) | copy-done | bytes 3145752
  68.2 2.8 %collective-permute-done.16.refs_4_ = bf16[272,256]{1,0:T(8,128)(2,1)S(1)} collective-permute-done((bf16[272,256]{1,0:T(8,128)(2,1)}, bf16[272,256]{1,0:T(8,128)(2,1)S(1)}, u32[]{:S(2)}, u32[]{:S(2)}) %collective-permute-start.16) | collective-permute-done | bytes 139296 | tf_op jit(solution)/shard_map/ppermute | solution.py:510
  71.0 2.0 %collective-permute-done.17.refs_5_ = bf16[272,256]{1,0:T(8,128)(2,1)S(1)} collective-permute-done((bf16[272,256]{1,0:T(8,128)(2,1)}, bf16[272,256]{1,0:T(8,128)(2,1)S(1)}, u32[]{:S(2)}, u32[]{:S(2)}) %collective-permute-start.17) | collective-permute-done | bytes 139296 | tf_op jit(solution)/shard_map/ppermute | solution.py:510
  74.4 9.5 %all-to-all-done.1.q_ref.acts_ref.kv_ref = bf16[16,640,128]{2,1,0:T(8,128)(2,1)S(1)} async-done(((bf16[16,640,128]{2,1,0:T(8,128)(2,1)}), bf16[16,640,128]{2,1,0:T(8,128)(2,1)S(1)}, u32[]{:S(2)}, u32[]{:S(2)}) %all-to-all-start.1) | async-done | bytes 2621472 | tf_op jit(solution)/shard_map/all_to_all | solution.py:452
  83.8 4.5 %all-to-all-start.2 = ((bf16[16,256,128]{2,1,0:T(8,128)(2,1)}), bf16[16,256,128]{2,1,0:T(8,128)(2,1)}, u32[]{:S(2)}, u32[]{:S(2)}) async-start(bf16[16,256,128]{2,1,0:T(8,128)(2,1)} %shard_map.105), calls=%async_computation.2 | async-start | bytes 2097152 | tf_op jit(solution)/shard_map/all_to_all | solution.py:452
  88.4 31.7 %shard_map.104 = (bf16[16,256,128]{2,1,0:T(8,128)(2,1)}, f32[4,128,1024]{2,1,0:T(8,128)}, f32[4,16,1024]{2,1,0:T(8,128)}, f32[4,128,1024]{2,1,0:T(8,128)}) custom-call(s32[1]{0:T(128)} %bitcast.here_ref, s32[8]{0:T(128)} %index_ref.5, s32[8]{0:T(128)} %rank_ref.3, bf16[16,640,128]{2,1,0:T(8,128)(2,1)} %copy-done.8, bf16[16,640,128]{2,1,0:T(8,128)(2,1)} %copy-done.8, ...), custom_call_target="tpu_custom_call" | custom-call | flops 8589934592 | bytes 8388608 | tf_op jit(solution)/shard_map/pallas_call | solution.py:396
  120.1 24.1 %shard_map.106 = bf16[16,256,128]{2,1,0:T(8,128)(2,1)} custom-call(bf16[16,256,128]{2,1,0:T(8,128)(2,1)} %get-tuple-element.28.q_ref, bf16[16,256,128]{2,1,0:T(8,128)(2,1)} %all-to-all-done.2.kv_ref, f32[4,128,1024]{2,1,0:T(8,128)} %get-tuple-element.30.acc_ref, f32[4,16,1024]{2,1,0:T(8,128)} %get-tuple-element.31.sums_ref, ...), custom_call_target="tpu_custom_call" | custom-call | flops 4294967296 | bytes 8388608 | tf_op jit(solution)/shard_map/pallas_call | solution.py:428
  144.3 19.9 %all_to_all.20.x_ref = bf16[16,256,128]{2,1,0:T(8,128)(2,1)S(1)} all-to-all(bf16[16,256,128]{2,1,0:T(8,128)(2,1)} %shard_map.106), channel_id=1, replica_groups=mesh['req'=8,'sp'=16] {'sp'}, dimensions={0} | all-to-all | bytes 2097152 | tf_op jit(solution)/shard_map/all_to_all | solution.py:452
  (76 shorter events, 19.9 us)
Async XLA Ops:
  2.3 2.4 %collective-permute-start = (bf16[2,64,3200]{2,1,0:T(8,128)(2,1)S(1)}, bf16[2,64,3200]{2,1,0:T(8,128)(2,1)S(1)}, u32[]{:S(2)}, u32[]{:S(2)}) collective-permute-start(bf16[2,64,3200]{2,1,0:T(8,128)(2,1)S(1)} %pad_maximum_fusion.own_ref), channel_id=1, source_target_pairs={{0,16},{16,0},{32,48},{48,32},{64,80},{80,64},{96,112},{112,96},{1... | collective-permute-start | bytes 2457608 | tf_op jit(solution)/shard_map/ppermute | solution.py:483
  7.1 33.3 %all-to-all-start = ((bf16[4,64,3200]{2,1,0:T(8,128)(2,1)}), bf16[4,64,3200]{2,1,0:T(8,128)(2,1)S(1)}, u32[]{:S(2)}, u32[]{:S(2)}) async-start(bf16[4,64,3200]{2,1,0:T(8,128)(2,1)} %shard_map.100), calls=%async_computation | async-start | bytes 3276800 | tf_op jit(solution)/shard_map/all_to_all | solution.py:495
  11.8 8.6 %collective-permute-start.3 = (bf16[4,8,1152]{2,1,0:T(8,128)(2,1)S(1)}, bf16[4,8,1152]{2,1,0:T(8,128)(2,1)S(1)}, u32[]{:S(2)}, u32[]{:S(2)}) collective-permute-start(bf16[4,8,1152]{2,1,0:T(8,128)(2,1)S(1)} %get-tuple-element.36), channel_id=1, source_target_pairs={{0,3},{1,0},{2,1},{3,2},{4,7},{5,4},{6,5},{7,6},{8,11},{9,8},{10,9... | collective-permute-start | bytes 221192 | tf_op jit(solution)/shard_map/ppermute | solution.py:488
  14.7 7.0 %collective-permute-start.2 = (bf16[4,8,1152]{2,1,0:T(8,128)(2,1)S(1)}, bf16[4,8,1152]{2,1,0:T(8,128)(2,1)S(1)}, u32[]{:S(2)}, u32[]{:S(2)}) collective-permute-start(bf16[4,8,1152]{2,1,0:T(8,128)(2,1)S(1)} %get-tuple-element.36), channel_id=1, source_target_pairs={{0,2},{1,3},{2,0},{3,1},{4,6},{5,7},{6,4},{7,5},{8,10},{9,11},{10,... | collective-permute-start | bytes 221192 | tf_op jit(solution)/shard_map/ppermute | solution.py:488
  15.5 6.2 %collective-permute-start.1 = (bf16[4,8,1152]{2,1,0:T(8,128)(2,1)S(1)}, bf16[4,8,1152]{2,1,0:T(8,128)(2,1)S(1)}, u32[]{:S(2)}, u32[]{:S(2)}) collective-permute-start(bf16[4,8,1152]{2,1,0:T(8,128)(2,1)S(1)} %get-tuple-element.36), channel_id=1, source_target_pairs={{0,1},{1,2},{2,3},{3,0},{4,5},{5,6},{6,7},{7,4},{8,9},{9,10},{10,1... | collective-permute-start | bytes 221192 | tf_op jit(solution)/shard_map/ppermute | solution.py:488
  16.4 10.8 %collective-permute-start.9 = (bf16[4,8,1152]{2,1,0:T(8,128)(2,1)S(1)}, bf16[4,8,1152]{2,1,0:T(8,128)(2,1)S(1)}, u32[]{:S(2)}, u32[]{:S(2)}) collective-permute-start(bf16[4,8,1152]{2,1,0:T(8,128)(2,1)S(1)} %get-tuple-element.35), channel_id=1, source_target_pairs={{0,12},{1,13},{2,14},{3,15},{4,0},{5,1},{6,2},{7,3},{8,4},{9,5},{1... | collective-permute-start | bytes 221192 | tf_op jit(solution)/shard_map/ppermute | solution.py:488
  20.4 7.8 %collective-permute-start.8 = (bf16[4,8,1152]{2,1,0:T(8,128)(2,1)S(1)}, bf16[4,8,1152]{2,1,0:T(8,128)(2,1)S(1)}, u32[]{:S(2)}, u32[]{:S(2)}) collective-permute-start(bf16[4,8,1152]{2,1,0:T(8,128)(2,1)S(1)} %get-tuple-element.35), channel_id=1, source_target_pairs={{0,8},{1,9},{2,10},{3,11},{4,12},{5,13},{6,14},{7,15},{8,0},{9,1},... | collective-permute-start | bytes 221192 | tf_op jit(solution)/shard_map/ppermute | solution.py:488
  20.4 7.8 %collective-permute-start.7 = (bf16[4,8,1152]{2,1,0:T(8,128)(2,1)S(1)}, bf16[4,8,1152]{2,1,0:T(8,128)(2,1)S(1)}, u32[]{:S(2)}, u32[]{:S(2)}) collective-permute-start(bf16[4,8,1152]{2,1,0:T(8,128)(2,1)S(1)} %get-tuple-element.35), channel_id=1, source_target_pairs={{0,4},{1,5},{2,6},{3,7},{4,8},{5,9},{6,10},{7,11},{8,12},{9,13},{1... | collective-permute-start | bytes 221192 | tf_op jit(solution)/shard_map/ppermute | solution.py:488
  21.7 18.7 %copy-start.9 = (bf16[4,4,8,1152]{3,2,1,0:T(8,128)(2,1)}, bf16[4,4,8,1152]{3,2,1,0:T(8,128)(2,1)S(1)}, u32[]{:S(2)}) copy-start(bf16[4,4,8,1152]{3,2,1,0:T(8,128)(2,1)S(1)} %pad_maximum_fusion.1) | copy-start | bytes 884740
  21.7 12.7 %collective-permute-start.4 = (bf16[128,1152]{1,0:T(8,128)(2,1)S(1)}, bf16[128,1152]{1,0:T(8,128)(2,1)S(1)}, u32[]{:S(2)}, u32[]{:S(2)}) collective-permute-start(bf16[128,1152]{1,0:T(8,128)(2,1)S(1)} %bitcast.25), channel_id=1, source_target_pairs={{0,4},{1,5},{2,6},{3,7},{4,8},{5,9},{6,10},{7,11},{8,12},{9,13},{1... | collective-permute-start | bytes 884744 | tf_op jit(solution)/shard_map/ppermute | solution.py:492
  24.0 20.6 %collective-permute-start.5 = (bf16[128,1152]{1,0:T(8,128)(2,1)S(1)}, bf16[128,1152]{1,0:T(8,128)(2,1)S(1)}, u32[]{:S(2)}, u32[]{:S(2)}) collective-permute-start(bf16[128,1152]{1,0:T(8,128)(2,1)S(1)} %bitcast.26), channel_id=1, source_target_pairs={{0,8},{1,9},{2,10},{3,11},{4,12},{5,13},{6,14},{7,15},{8,0},{9,1},... | collective-permute-start | bytes 884744 | tf_op jit(solution)/shard_map/ppermute | solution.py:492
  27.1 17.5 %collective-permute-start.6 = (bf16[128,1152]{1,0:T(8,128)(2,1)S(1)}, bf16[128,1152]{1,0:T(8,128)(2,1)}, u32[]{:S(2)}, u32[]{:S(2)}) collective-permute-start(bf16[128,1152]{1,0:T(8,128)(2,1)S(1)} %bitcast.27), channel_id=1, source_target_pairs={{0,12},{1,13},{2,14},{3,15},{4,0},{5,1},{6,2},{7,3},{8,4},{9,5},{1... | collective-permute-start | bytes 884744 | tf_op jit(solution)/shard_map/ppermute | solution.py:492
  28.2 16.4 %collective-permute-start.10 = (bf16[128,1152]{1,0:T(8,128)(2,1)S(1)}, bf16[128,1152]{1,0:T(8,128)(2,1)}, u32[]{:S(2)}, u32[]{:S(2)}) collective-permute-start(bf16[128,1152]{1,0:T(8,128)(2,1)S(1)} %bitcast.29), channel_id=1, source_target_pairs={{0,1},{1,2},{2,3},{3,0},{4,5},{5,6},{6,7},{7,4},{8,9},{9,10},{10,1... | collective-permute-start | bytes 884744 | tf_op jit(solution)/shard_map/ppermute | solution.py:492
  29.5 15.1 %collective-permute-start.11 = (bf16[128,1152]{1,0:T(8,128)(2,1)S(1)}, bf16[128,1152]{1,0:T(8,128)(2,1)}, u32[]{:S(2)}, u32[]{:S(2)}) collective-permute-start(bf16[128,1152]{1,0:T(8,128)(2,1)S(1)} %bitcast.30), channel_id=1, source_target_pairs={{0,2},{1,3},{2,0},{3,1},{4,6},{5,7},{6,4},{7,5},{8,10},{9,11},{10,... | collective-permute-start | bytes 884744 | tf_op jit(solution)/shard_map/ppermute | solution.py:492
  34.5 10.2 %collective-permute-start.12 = (bf16[128,1152]{1,0:T(8,128)(2,1)S(1)}, bf16[128,1152]{1,0:T(8,128)(2,1)}, u32[]{:S(2)}, u32[]{:S(2)}) collective-permute-start(bf16[128,1152]{1,0:T(8,128)(2,1)S(1)} %bitcast.31), channel_id=1, source_target_pairs={{0,3},{1,0},{2,1},{3,2},{4,7},{5,4},{6,5},{7,6},{8,11},{9,8},{10,9... | collective-permute-start | bytes 884744 | tf_op jit(solution)/shard_map/ppermute | solution.py:492
  45.3 38.5 %all-to-all-start.1 = ((bf16[16,640,128]{2,1,0:T(8,128)(2,1)}), bf16[16,640,128]{2,1,0:T(8,128)(2,1)S(1)}, u32[]{:S(2)}, u32[]{:S(2)}) async-start(bf16[16,640,128]{2,1,0:T(8,128)(2,1)} %shard_map.102), calls=%async_computation.1 | async-start | bytes 5242880 | tf_op jit(solution)/shard_map/all_to_all | solution.py:452
  57.1 5.1 %collective-permute-start.13 = (bf16[272,256]{1,0:T(8,128)(2,1)}, bf16[272,256]{1,0:T(8,128)(2,1)S(1)}, u32[]{:S(2)}, u32[]{:S(2)}) collective-permute-start(bf16[272,256]{1,0:T(8,128)(2,1)} %get-tuple-element.21), channel_id=1, source_target_pairs={{0,16},{16,0},{32,48},{48,32},{64,80},{80,64},{96,112},{112,96},{1... | collective-permute-start | bytes 417800 | tf_op jit(solution)/shard_map/ppermute | solution.py:510
  57.1 8.0 %collective-permute-start.14 = (bf16[272,256]{1,0:T(8,128)(2,1)}, bf16[272,256]{1,0:T(8,128)(2,1)S(1)}, u32[]{:S(2)}, u32[]{:S(2)}) collective-permute-start(bf16[272,256]{1,0:T(8,128)(2,1)} %get-tuple-element.22), channel_id=1, source_target_pairs={{0,32},{16,48},{32,64},{48,80},{64,96},{80,112},{96,0},{112,16},{1... | collective-permute-start | bytes 417800 | tf_op jit(solution)/shard_map/ppermute | solution.py:510
  57.7 10.5 %collective-permute-start.15 = (bf16[272,256]{1,0:T(8,128)(2,1)}, bf16[272,256]{1,0:T(8,128)(2,1)S(1)}, u32[]{:S(2)}, u32[]{:S(2)}) collective-permute-start(bf16[272,256]{1,0:T(8,128)(2,1)} %get-tuple-element.23), channel_id=1, source_target_pairs={{0,48},{16,32},{32,80},{48,64},{64,112},{80,96},{96,16},{112,0},{1... | collective-permute-start | bytes 417800 | tf_op jit(solution)/shard_map/ppermute | solution.py:510
  58.9 12.1 %collective-permute-start.16 = (bf16[272,256]{1,0:T(8,128)(2,1)}, bf16[272,256]{1,0:T(8,128)(2,1)S(1)}, u32[]{:S(2)}, u32[]{:S(2)}) collective-permute-start(bf16[272,256]{1,0:T(8,128)(2,1)} %get-tuple-element.24), channel_id=1, source_target_pairs={{0,64},{16,80},{32,96},{48,112},{64,0},{80,16},{96,32},{112,48},{1... | collective-permute-start | bytes 417800 | tf_op jit(solution)/shard_map/ppermute | solution.py:510
  61.6 11.5 %collective-permute-start.17 = (bf16[272,256]{1,0:T(8,128)(2,1)}, bf16[272,256]{1,0:T(8,128)(2,1)S(1)}, u32[]{:S(2)}, u32[]{:S(2)}) collective-permute-start(bf16[272,256]{1,0:T(8,128)(2,1)} %get-tuple-element.25), channel_id=1, source_target_pairs={{0,80},{16,64},{32,112},{48,96},{64,16},{80,0},{96,48},{112,32},{1... | collective-permute-start | bytes 417800 | tf_op jit(solution)/shard_map/ppermute | solution.py:510
  62.1 10.9 %collective-permute-start.18 = (bf16[272,256]{1,0:T(8,128)(2,1)}, bf16[272,256]{1,0:T(8,128)(2,1)S(1)}, u32[]{:S(2)}, u32[]{:S(2)}) collective-permute-start(bf16[272,256]{1,0:T(8,128)(2,1)} %get-tuple-element.26), channel_id=1, source_target_pairs={{0,96},{16,112},{32,0},{48,16},{64,32},{80,48},{96,64},{112,80},{1... | collective-permute-start | bytes 417800 | tf_op jit(solution)/shard_map/ppermute | solution.py:510
  65.0 9.3 %collective-permute-start.19 = (bf16[272,256]{1,0:T(8,128)(2,1)}, bf16[272,256]{1,0:T(8,128)(2,1)}, u32[]{:S(2)}, u32[]{:S(2)}) collective-permute-start(bf16[272,256]{1,0:T(8,128)(2,1)} %get-tuple-element.27), channel_id=1, source_target_pairs={{0,112},{16,96},{32,16},{48,0},{64,48},{80,32},{96,80},{112,64},{1... | collective-permute-start | bytes 417800 | tf_op jit(solution)/shard_map/ppermute | solution.py:510
  83.8 36.3 %all-to-all-start.2 = ((bf16[16,256,128]{2,1,0:T(8,128)(2,1)}), bf16[16,256,128]{2,1,0:T(8,128)(2,1)}, u32[]{:S(2)}, u32[]{:S(2)}) async-start(bf16[16,256,128]{2,1,0:T(8,128)(2,1)} %shard_map.105), calls=%async_computation.2 | async-start | bytes 2097152 | tf_op jit(solution)/shard_map/all_to_all | solution.py:452
  (19 other events, 60.7 us)

commit v4 on v3

--- a/solution.py
+++ b/solution.py
@@ -373,7 +373,7 @@
         emit(*self_part_by_maximum(kv_ref, q_ref[...].reshape(per_step * TOK, HD), chunk))
 
 
-PER_STEP, CHUNK = 4, 1024
+PER_STEP, CHUNK = 4, 2048
 STEPS = HEADS // PER_STEP
 HEAD_BLOCK = pl.BlockSpec((PER_STEP, TOK, HD), lambda i: (i, 0, 0))
 KEYS_BLOCK = pl.BlockSpec((HEADS, TOK, HD), lambda i: (0, 0, 0))

time: 166 us -> 165 us (level)
  transfers between devices with their start and end apart: 23 -> 23, of which waited for: 6 -> 6; matrix products, arithmetic and copies ran while one was open for 0% -> 0% of each run, Pallas kernels for 25% -> 24%
where the time goes in v4:
time: 165 us
  Pallas kernels  67 us (41%)
  starting transfers between devices  46 us (28%)
  waiting for transfers between devices  20.8 us (13%)
  blocking collectives  19.9 us (12%)
  local copies, waits for them, and re-layouts  9.51 us (6%)
    pallas_call x1, Pallas kernels, attend_first(): pl.pallas_call(functools.partial(first_kernel, per_step=PER_STEP, chunk=C...  31.3 us
    pallas_call x1, Pallas kernels, attend_second(): pl.pallas_call(functools.partial(second_kernel, per_step=PER_STEP, chunk=...  23.9 us
    all_to_all x1, blocking collectives, exchange(): return lax.all_to_all(x, 'sp', split_axis=0, concat_axis=0, tiled=True)  19.9 us
    all_to_all x2, starting transfers between devices, exchange(): return lax.all_to_all(x, 'sp', split_axis=0, concat_axis=0, tiled=True)  12.4 us
    ppermute x6, starting transfers between devices, shards(): pieces += [line] + [lax.ppermute(line, 'sp', way(k)) for k in (1, 2, 3)]  12.1 us
    ppermute x6, starting transfers between devices, shards(): line = [part] + [lax.ppermute(part, 'sp', way(k)) for k in (1, 2, 3)]  9.81 us
    all_to_all x2, waiting for transfers between devices, exchange(): return lax.all_to_all(x, 'sp', split_axis=0, concat_axis=0, tiled=True)  9.49 us
    unnamed x40, local copies, waits for them, and re-layouts  9.47 us
  transfers between devices with their start and end apart: 23, of which 6 were waited for; matrix products, arithmetic and copies ran while one was open for 0% of the time, Pallas kernels for 24%

profile of v4, /device:TPU:0, one launch (start us, length us, event | category | flops | bytes accessed | tf_op | source)
XLA Modules:
  0.0 164.7 jit_solution(1963916410720872983)
XLA Ops:
  2.4 2.3 %collective-permute-done.other_ref = bf16[2,64,3200]{2,1,0:T(8,128)(2,1)S(1)} collective-permute-done((bf16[2,64,3200]{2,1,0:T(8,128)(2,1)S(1)}, bf16[2,64,3200]{2,1,0:T(8,128)(2,1)S(1)}, u32[]{:S(2)}, u32[]{:S(2)}) %collective-permute-start) | collective-permute-done | bytes 819232 | tf_op jit(solution)/shard_map/ppermute | solution.py:483
  5.3 1.8 %shard_map.100 = bf16[4,64,3200]{2,1,0:T(8,128)(2,1)} custom-call(s32[1]{0:T(128)} %bitcast.here_ref, s32[8]{0:T(128)S(1)} %copy-done.5, bf16[2,64,3200]{2,1,0:T(8,128)(2,1)S(1)} %pad_maximum_fusion.own_ref, bf16[2,64,3200]{2,1,0:T(8,128)(2,1)S(1)} %collective-permute-done.other_ref), custom_call_target="tpu_custom_call" | custom-call | bytes 3276800 | tf_op jit(solution)/shard_map/pallas_call | solution.py:109
  7.1 4.7 %all-to-all-start = ((bf16[4,64,3200]{2,1,0:T(8,128)(2,1)}), bf16[4,64,3200]{2,1,0:T(8,128)(2,1)S(1)}, u32[]{:S(2)}, u32[]{:S(2)}) async-start(bf16[4,64,3200]{2,1,0:T(8,128)(2,1)} %shard_map.100), calls=%async_computation | async-start | bytes 3276800 | tf_op jit(solution)/shard_map/all_to_all | solution.py:495
  11.8 2.8 %collective-permute-start.3 = (bf16[4,8,1152]{2,1,0:T(8,128)(2,1)S(1)}, bf16[4,8,1152]{2,1,0:T(8,128)(2,1)S(1)}, u32[]{:S(2)}, u32[]{:S(2)}) collective-permute-start(bf16[4,8,1152]{2,1,0:T(8,128)(2,1)S(1)} %get-tuple-element.36), channel_id=1, source_target_pairs={{0,3},{1,0},{2,1},{3,2},{4,7},{5,4},{6,5},{7,6},{8,11},{9,8},{10,9... | collective-permute-start | bytes 221192 | tf_op jit(solution)/shard_map/ppermute | solution.py:488
  16.4 4.0 %collective-permute-start.9 = (bf16[4,8,1152]{2,1,0:T(8,128)(2,1)S(1)}, bf16[4,8,1152]{2,1,0:T(8,128)(2,1)S(1)}, u32[]{:S(2)}, u32[]{:S(2)}) collective-permute-start(bf16[4,8,1152]{2,1,0:T(8,128)(2,1)S(1)} %get-tuple-element.35), channel_id=1, source_target_pairs={{0,12},{1,13},{2,14},{3,15},{4,0},{5,1},{6,2},{7,3},{8,4},{9,5},{1... | collective-permute-start | bytes 221192 | tf_op jit(solution)/shard_map/ppermute | solution.py:488
  21.7 2.3 %collective-permute-start.4 = (bf16[128,1152]{1,0:T(8,128)(2,1)S(1)}, bf16[128,1152]{1,0:T(8,128)(2,1)S(1)}, u32[]{:S(2)}, u32[]{:S(2)}) collective-permute-start(bf16[128,1152]{1,0:T(8,128)(2,1)S(1)} %bitcast.25), channel_id=1, source_target_pairs={{0,4},{1,5},{2,6},{3,7},{4,8},{5,9},{6,10},{7,11},{8,12},{9,13},{1... | collective-permute-start | bytes 884744 | tf_op jit(solution)/shard_map/ppermute | solution.py:492
  24.0 3.1 %collective-permute-start.5 = (bf16[128,1152]{1,0:T(8,128)(2,1)S(1)}, bf16[128,1152]{1,0:T(8,128)(2,1)S(1)}, u32[]{:S(2)}, u32[]{:S(2)}) collective-permute-start(bf16[128,1152]{1,0:T(8,128)(2,1)S(1)} %bitcast.26), channel_id=1, source_target_pairs={{0,8},{1,9},{2,10},{3,11},{4,12},{5,13},{6,14},{7,15},{8,0},{9,1},... | collective-permute-start | bytes 884744 | tf_op jit(solution)/shard_map/ppermute | solution.py:492
  29.5 2.0 %collective-permute-start.11 = (bf16[128,1152]{1,0:T(8,128)(2,1)S(1)}, bf16[128,1152]{1,0:T(8,128)(2,1)}, u32[]{:S(2)}, u32[]{:S(2)}) collective-permute-start(bf16[128,1152]{1,0:T(8,128)(2,1)S(1)} %bitcast.30), channel_id=1, source_target_pairs={{0,2},{1,3},{2,0},{3,1},{4,6},{5,7},{6,4},{7,5},{8,10},{9,11},{10,... | collective-permute-start | bytes 884744 | tf_op jit(solution)/shard_map/ppermute | solution.py:492
  31.5 2.9 %collective-permute-done.4.refs_1_ = bf16[128,1152]{1,0:T(8,128)(2,1)S(1)} collective-permute-done((bf16[128,1152]{1,0:T(8,128)(2,1)S(1)}, bf16[128,1152]{1,0:T(8,128)(2,1)S(1)}, u32[]{:S(2)}, u32[]{:S(2)}) %collective-permute-start.4) | collective-permute-done | bytes 294944 | tf_op jit(solution)/shard_map/ppermute | solution.py:492
  34.5 2.3 %collective-permute-start.12 = (bf16[128,1152]{1,0:T(8,128)(2,1)S(1)}, bf16[128,1152]{1,0:T(8,128)(2,1)}, u32[]{:S(2)}, u32[]{:S(2)}) collective-permute-start(bf16[128,1152]{1,0:T(8,128)(2,1)S(1)} %bitcast.31), channel_id=1, source_target_pairs={{0,3},{1,0},{2,1},{3,2},{4,7},{5,4},{6,5},{7,6},{8,11},{9,8},{10,9... | collective-permute-start | bytes 884744 | tf_op jit(solution)/shard_map/ppermute | solution.py:492
  36.8 1.9 %copy-done.1 = bf16[1,256,3,2048]{3,1,2,0:T(8,128)(2,1)S(1)} copy-done((bf16[1,256,3,2048]{3,1,2,0:T(8,128)(2,1)S(1)}, bf16[1,256,3,2048]{3,1,2,0:T(8,128)(2,1)}, u32[]{:S(2)}) %copy-start.1) | copy-done | bytes 3145752
  40.5 2.0 %copy-done.4 = bf16[1,256,3072]{2,1,0:T(8,128)(2,1)S(1)} copy-done((bf16[1,256,3072]{2,1,0:T(8,128)(2,1)S(1)}, bf16[1,256,3072]{2,1,0:T(8,128)(2,1)}, u32[]{:S(2)}) %copy-start.4) | copy-done | bytes 1572888
  42.4 2.1 %shard_map.102 = bf16[16,640,128]{2,1,0:T(8,128)(2,1)} custom-call(s32[1]{0:T(128)} %bitcast.here_ref, s32[8]{0:T(128)S(1)} %copy-done.6, s32[8]{0:T(128)S(1)} %copy-done.7, bf16[256,3072]{1,0:T(8,128)(2,1)S(1)} %bitcast.24, bf16[4,64,3200]{2,1,0:T(8,128)(2,1)S(1)} %all-to-all-done.a_ref.up_ref, ...), custom_call_target="tpu_custom_call", output_to_operand_aliasing={{}: (5, {})} | custom-call | flops 100663296 | bytes 4194304 | tf_op jit(solution)/shard_map/pallas_call | solution.py:141
  45.3 7.9 %all-to-all-start.1 = ((bf16[16,640,128]{2,1,0:T(8,128)(2,1)}), bf16[16,640,128]{2,1,0:T(8,128)(2,1)S(1)}, u32[]{:S(2)}, u32[]{:S(2)}) async-start(bf16[16,640,128]{2,1,0:T(8,128)(2,1)} %shard_map.102), calls=%async_computation.1 | async-start | bytes 5242880 | tf_op jit(solution)/shard_map/all_to_all | solution.py:452
  53.2 3.8 %shard_map.103 = (bf16[272,256]{1,0:T(8,128)(2,1)}, bf16[272,256]{1,0:T(8,128)(2,1)}, bf16[272,256]{1,0:T(8,128)(2,1)}, bf16[272,256]{1,0:T(8,128)(2,1)}, bf16[2...) custom-call(s32[1]{0:T(128)} %bitcast.here_ref, ...), custom_call_target="tpu_custom_call" | custom-call | flops 603979776 | bytes 5242880 | tf_op jit(solution)/shard_map/pallas_call | solution.py:190
  58.9 2.7 %collective-permute-start.16 = (bf16[272,256]{1,0:T(8,128)(2,1)}, bf16[272,256]{1,0:T(8,128)(2,1)S(1)}, u32[]{:S(2)}, u32[]{:S(2)}) collective-permute-start(bf16[272,256]{1,0:T(8,128)(2,1)} %get-tuple-element.24), channel_id=1, source_target_pairs={{0,64},{16,80},{32,96},{48,112},{64,0},{80,16},{96,32},{112,48},{1... | collective-permute-start | bytes 417800 | tf_op jit(solution)/shard_map/ppermute | solution.py:510
  65.1 1.9 %copy-done.2 = bf16[1,256,3,2048]{3,1,2,0:T(8,128)(2,1)S(1)} copy-done((bf16[1,256,3,2048]{3,1,2,0:T(8,128)(2,1)S(1)}, bf16[1,256,3,2048]{3,1,2,0:T(8,128)(2,1)}, u32[]{:S(2)}) %copy-start.2) | copy-done | bytes 3145752
  68.2 2.8 %collective-permute-done.16.refs_4_ = bf16[272,256]{1,0:T(8,128)(2,1)S(1)} collective-permute-done((bf16[272,256]{1,0:T(8,128)(2,1)}, bf16[272,256]{1,0:T(8,128)(2,1)S(1)}, u32[]{:S(2)}, u32[]{:S(2)}) %collective-permute-start.16) | collective-permute-done | bytes 139296 | tf_op jit(solution)/shard_map/ppermute | solution.py:510
  71.0 2.0 %collective-permute-done.17.refs_5_ = bf16[272,256]{1,0:T(8,128)(2,1)S(1)} collective-permute-done((bf16[272,256]{1,0:T(8,128)(2,1)}, bf16[272,256]{1,0:T(8,128)(2,1)S(1)}, u32[]{:S(2)}, u32[]{:S(2)}) %collective-permute-start.17) | collective-permute-done | bytes 139296 | tf_op jit(solution)/shard_map/ppermute | solution.py:510
  74.4 9.5 %all-to-all-done.1.q_ref.acts_ref.kv_ref = bf16[16,640,128]{2,1,0:T(8,128)(2,1)S(1)} async-done(((bf16[16,640,128]{2,1,0:T(8,128)(2,1)}), bf16[16,640,128]{2,1,0:T(8,128)(2,1)S(1)}, u32[]{:S(2)}, u32[]{:S(2)}) %all-to-all-start.1) | async-done | bytes 2621472 | tf_op jit(solution)/shard_map/all_to_all | solution.py:452
  83.9 4.5 %all-to-all-start.2 = ((bf16[16,256,128]{2,1,0:T(8,128)(2,1)}), bf16[16,256,128]{2,1,0:T(8,128)(2,1)}, u32[]{:S(2)}, u32[]{:S(2)}) async-start(bf16[16,256,128]{2,1,0:T(8,128)(2,1)} %shard_map.105), calls=%async_computation.2 | async-start | bytes 2097152 | tf_op jit(solution)/shard_map/all_to_all | solution.py:452
  88.4 31.3 %shard_map.104 = (bf16[16,256,128]{2,1,0:T(8,128)(2,1)}, f32[4,128,1024]{2,1,0:T(8,128)}, f32[4,16,1024]{2,1,0:T(8,128)}, f32[4,128,1024]{2,1,0:T(8,128)}) custom-call(s32[1]{0:T(128)} %bitcast.here_ref, s32[8]{0:T(128)} %index_ref.5, s32[8]{0:T(128)} %rank_ref.3, bf16[16,640,128]{2,1,0:T(8,128)(2,1)} %copy-done.8, bf16[16,640,128]{2,1,0:T(8,128)(2,1)} %copy-done.8, ...), custom_call_target="tpu_custom_call" | custom-call | flops 8589934592 | bytes 8388608 | tf_op jit(solution)/shard_map/pallas_call | solution.py:396
  119.7 23.9 %shard_map.106 = bf16[16,256,128]{2,1,0:T(8,128)(2,1)} custom-call(bf16[16,256,128]{2,1,0:T(8,128)(2,1)} %get-tuple-element.28.q_ref, bf16[16,256,128]{2,1,0:T(8,128)(2,1)} %all-to-all-done.2.kv_ref, f32[4,128,1024]{2,1,0:T(8,128)} %get-tuple-element.30.acc_ref, f32[4,16,1024]{2,1,0:T(8,128)} %get-tuple-element.31.sums_ref, ...), custom_call_target="tpu_custom_call" | custom-call | flops 4294967296 | bytes 8388608 | tf_op jit(solution)/shard_map/pallas_call | solution.py:428
  143.6 19.9 %all_to_all.20.x_ref = bf16[16,256,128]{2,1,0:T(8,128)(2,1)S(1)} all-to-all(bf16[16,256,128]{2,1,0:T(8,128)(2,1)} %shard_map.106), channel_id=1, replica_groups=mesh['req'=8,'sp'=16] {'sp'}, dimensions={0} | all-to-all | bytes 2097152 | tf_op jit(solution)/shard_map/all_to_all | solution.py:452
  (76 shorter events, 19.9 us)
Async XLA Ops:
  2.3 2.4 %collective-permute-start = (bf16[2,64,3200]{2,1,0:T(8,128)(2,1)S(1)}, bf16[2,64,3200]{2,1,0:T(8,128)(2,1)S(1)}, u32[]{:S(2)}, u32[]{:S(2)}) collective-permute-start(bf16[2,64,3200]{2,1,0:T(8,128)(2,1)S(1)} %pad_maximum_fusion.own_ref), channel_id=1, source_target_pairs={{0,16},{16,0},{32,48},{48,32},{64,80},{80,64},{96,112},{112,96},{1... | collective-permute-start | bytes 2457608 | tf_op jit(solution)/shard_map/ppermute | solution.py:483
  7.1 33.3 %all-to-all-start = ((bf16[4,64,3200]{2,1,0:T(8,128)(2,1)}), bf16[4,64,3200]{2,1,0:T(8,128)(2,1)S(1)}, u32[]{:S(2)}, u32[]{:S(2)}) async-start(bf16[4,64,3200]{2,1,0:T(8,128)(2,1)} %shard_map.100), calls=%async_computation | async-start | bytes 3276800 | tf_op jit(solution)/shard_map/all_to_all | solution.py:495
  11.8 8.6 %collective-permute-start.3 = (bf16[4,8,1152]{2,1,0:T(8,128)(2,1)S(1)}, bf16[4,8,1152]{2,1,0:T(8,128)(2,1)S(1)}, u32[]{:S(2)}, u32[]{:S(2)}) collective-permute-start(bf16[4,8,1152]{2,1,0:T(8,128)(2,1)S(1)} %get-tuple-element.36), channel_id=1, source_target_pairs={{0,3},{1,0},{2,1},{3,2},{4,7},{5,4},{6,5},{7,6},{8,11},{9,8},{10,9... | collective-permute-start | bytes 221192 | tf_op jit(solution)/shard_map/ppermute | solution.py:488
  14.7 7.0 %collective-permute-start.2 = (bf16[4,8,1152]{2,1,0:T(8,128)(2,1)S(1)}, bf16[4,8,1152]{2,1,0:T(8,128)(2,1)S(1)}, u32[]{:S(2)}, u32[]{:S(2)}) collective-permute-start(bf16[4,8,1152]{2,1,0:T(8,128)(2,1)S(1)} %get-tuple-element.36), channel_id=1, source_target_pairs={{0,2},{1,3},{2,0},{3,1},{4,6},{5,7},{6,4},{7,5},{8,10},{9,11},{10,... | collective-permute-start | bytes 221192 | tf_op jit(solution)/shard_map/ppermute | solution.py:488
  15.5 6.2 %collective-permute-start.1 = (bf16[4,8,1152]{2,1,0:T(8,128)(2,1)S(1)}, bf16[4,8,1152]{2,1,0:T(8,128)(2,1)S(1)}, u32[]{:S(2)}, u32[]{:S(2)}) collective-permute-start(bf16[4,8,1152]{2,1,0:T(8,128)(2,1)S(1)} %get-tuple-element.36), channel_id=1, source_target_pairs={{0,1},{1,2},{2,3},{3,0},{4,5},{5,6},{6,7},{7,4},{8,9},{9,10},{10,1... | collective-permute-start | bytes 221192 | tf_op jit(solution)/shard_map/ppermute | solution.py:488
  16.4 10.8 %collective-permute-start.9 = (bf16[4,8,1152]{2,1,0:T(8,128)(2,1)S(1)}, bf16[4,8,1152]{2,1,0:T(8,128)(2,1)S(1)}, u32[]{:S(2)}, u32[]{:S(2)}) collective-permute-start(bf16[4,8,1152]{2,1,0:T(8,128)(2,1)S(1)} %get-tuple-element.35), channel_id=1, source_target_pairs={{0,12},{1,13},{2,14},{3,15},{4,0},{5,1},{6,2},{7,3},{8,4},{9,5},{1... | collective-permute-start | bytes 221192 | tf_op jit(solution)/shard_map/ppermute | solution.py:488
  20.4 7.8 %collective-permute-start.8 = (bf16[4,8,1152]{2,1,0:T(8,128)(2,1)S(1)}, bf16[4,8,1152]{2,1,0:T(8,128)(2,1)S(1)}, u32[]{:S(2)}, u32[]{:S(2)}) collective-permute-start(bf16[4,8,1152]{2,1,0:T(8,128)(2,1)S(1)} %get-tuple-element.35), channel_id=1, source_target_pairs={{0,8},{1,9},{2,10},{3,11},{4,12},{5,13},{6,14},{7,15},{8,0},{9,1},... | collective-permute-start | bytes 221192 | tf_op jit(solution)/shard_map/ppermute | solution.py:488
  20.4 7.8 %collective-permute-start.7 = (bf16[4,8,1152]{2,1,0:T(8,128)(2,1)S(1)}, bf16[4,8,1152]{2,1,0:T(8,128)(2,1)S(1)}, u32[]{:S(2)}, u32[]{:S(2)}) collective-permute-start(bf16[4,8,1152]{2,1,0:T(8,128)(2,1)S(1)} %get-tuple-element.35), channel_id=1, source_target_pairs={{0,4},{1,5},{2,6},{3,7},{4,8},{5,9},{6,10},{7,11},{8,12},{9,13},{1... | collective-permute-start | bytes 221192 | tf_op jit(solution)/shard_map/ppermute | solution.py:488
  21.7 18.7 %copy-start.9 = (bf16[4,4,8,1152]{3,2,1,0:T(8,128)(2,1)}, bf16[4,4,8,1152]{3,2,1,0:T(8,128)(2,1)S(1)}, u32[]{:S(2)}) copy-start(bf16[4,4,8,1152]{3,2,1,0:T(8,128)(2,1)S(1)} %pad_maximum_fusion.1) | copy-start | bytes 884740
  21.7 12.7 %collective-permute-start.4 = (bf16[128,1152]{1,0:T(8,128)(2,1)S(1)}, bf16[128,1152]{1,0:T(8,128)(2,1)S(1)}, u32[]{:S(2)}, u32[]{:S(2)}) collective-permute-start(bf16[128,1152]{1,0:T(8,128)(2,1)S(1)} %bitcast.25), channel_id=1, source_target_pairs={{0,4},{1,5},{2,6},{3,7},{4,8},{5,9},{6,10},{7,11},{8,12},{9,13},{1... | collective-permute-start | bytes 884744 | tf_op jit(solution)/shard_map/ppermute | solution.py:492
  24.0 20.6 %collective-permute-start.5 = (bf16[128,1152]{1,0:T(8,128)(2,1)S(1)}, bf16[128,1152]{1,0:T(8,128)(2,1)S(1)}, u32[]{:S(2)}, u32[]{:S(2)}) collective-permute-start(bf16[128,1152]{1,0:T(8,128)(2,1)S(1)} %bitcast.26), channel_id=1, source_target_pairs={{0,8},{1,9},{2,10},{3,11},{4,12},{5,13},{6,14},{7,15},{8,0},{9,1},... | collective-permute-start | bytes 884744 | tf_op jit(solution)/shard_map/ppermute | solution.py:492
  27.1 17.5 %collective-permute-start.6 = (bf16[128,1152]{1,0:T(8,128)(2,1)S(1)}, bf16[128,1152]{1,0:T(8,128)(2,1)}, u32[]{:S(2)}, u32[]{:S(2)}) collective-permute-start(bf16[128,1152]{1,0:T(8,128)(2,1)S(1)} %bitcast.27), channel_id=1, source_target_pairs={{0,12},{1,13},{2,14},{3,15},{4,0},{5,1},{6,2},{7,3},{8,4},{9,5},{1... | collective-permute-start | bytes 884744 | tf_op jit(solution)/shard_map/ppermute | solution.py:492
  28.2 16.4 %collective-permute-start.10 = (bf16[128,1152]{1,0:T(8,128)(2,1)S(1)}, bf16[128,1152]{1,0:T(8,128)(2,1)}, u32[]{:S(2)}, u32[]{:S(2)}) collective-permute-start(bf16[128,1152]{1,0:T(8,128)(2,1)S(1)} %bitcast.29), channel_id=1, source_target_pairs={{0,1},{1,2},{2,3},{3,0},{4,5},{5,6},{6,7},{7,4},{8,9},{9,10},{10,1... | collective-permute-start | bytes 884744 | tf_op jit(solution)/shard_map/ppermute | solution.py:492
  29.5 15.1 %collective-permute-start.11 = (bf16[128,1152]{1,0:T(8,128)(2,1)S(1)}, bf16[128,1152]{1,0:T(8,128)(2,1)}, u32[]{:S(2)}, u32[]{:S(2)}) collective-permute-start(bf16[128,1152]{1,0:T(8,128)(2,1)S(1)} %bitcast.30), channel_id=1, source_target_pairs={{0,2},{1,3},{2,0},{3,1},{4,6},{5,7},{6,4},{7,5},{8,10},{9,11},{10,... | collective-permute-start | bytes 884744 | tf_op jit(solution)/shard_map/ppermute | solution.py:492
  34.5 10.2 %collective-permute-start.12 = (bf16[128,1152]{1,0:T(8,128)(2,1)S(1)}, bf16[128,1152]{1,0:T(8,128)(2,1)}, u32[]{:S(2)}, u32[]{:S(2)}) collective-permute-start(bf16[128,1152]{1,0:T(8,128)(2,1)S(1)} %bitcast.31), channel_id=1, source_target_pairs={{0,3},{1,0},{2,1},{3,2},{4,7},{5,4},{6,5},{7,6},{8,11},{9,8},{10,9... | collective-permute-start | bytes 884744 | tf_op jit(solution)/shard_map/ppermute | solution.py:492
  45.3 38.5 %all-to-all-start.1 = ((bf16[16,640,128]{2,1,0:T(8,128)(2,1)}), bf16[16,640,128]{2,1,0:T(8,128)(2,1)S(1)}, u32[]{:S(2)}, u32[]{:S(2)}) async-start(bf16[16,640,128]{2,1,0:T(8,128)(2,1)} %shard_map.102), calls=%async_computation.1 | async-start | bytes 5242880 | tf_op jit(solution)/shard_map/all_to_all | solution.py:452
  57.1 5.1 %collective-permute-start.13 = (bf16[272,256]{1,0:T(8,128)(2,1)}, bf16[272,256]{1,0:T(8,128)(2,1)S(1)}, u32[]{:S(2)}, u32[]{:S(2)}) collective-permute-start(bf16[272,256]{1,0:T(8,128)(2,1)} %get-tuple-element.21), channel_id=1, source_target_pairs={{0,16},{16,0},{32,48},{48,32},{64,80},{80,64},{96,112},{112,96},{1... | collective-permute-start | bytes 417800 | tf_op jit(solution)/shard_map/ppermute | solution.py:510
  57.1 8.0 %collective-permute-start.14 = (bf16[272,256]{1,0:T(8,128)(2,1)}, bf16[272,256]{1,0:T(8,128)(2,1)S(1)}, u32[]{:S(2)}, u32[]{:S(2)}) collective-permute-start(bf16[272,256]{1,0:T(8,128)(2,1)} %get-tuple-element.22), channel_id=1, source_target_pairs={{0,32},{16,48},{32,64},{48,80},{64,96},{80,112},{96,0},{112,16},{1... | collective-permute-start | bytes 417800 | tf_op jit(solution)/shard_map/ppermute | solution.py:510
  57.7 10.5 %collective-permute-start.15 = (bf16[272,256]{1,0:T(8,128)(2,1)}, bf16[272,256]{1,0:T(8,128)(2,1)S(1)}, u32[]{:S(2)}, u32[]{:S(2)}) collective-permute-start(bf16[272,256]{1,0:T(8,128)(2,1)} %get-tuple-element.23), channel_id=1, source_target_pairs={{0,48},{16,32},{32,80},{48,64},{64,112},{80,96},{96,16},{112,0},{1... | collective-permute-start | bytes 417800 | tf_op jit(solution)/shard_map/ppermute | solution.py:510
  58.9 12.1 %collective-permute-start.16 = (bf16[272,256]{1,0:T(8,128)(2,1)}, bf16[272,256]{1,0:T(8,128)(2,1)S(1)}, u32[]{:S(2)}, u32[]{:S(2)}) collective-permute-start(bf16[272,256]{1,0:T(8,128)(2,1)} %get-tuple-element.24), channel_id=1, source_target_pairs={{0,64},{16,80},{32,96},{48,112},{64,0},{80,16},{96,32},{112,48},{1... | collective-permute-start | bytes 417800 | tf_op jit(solution)/shard_map/ppermute | solution.py:510
  61.6 11.5 %collective-permute-start.17 = (bf16[272,256]{1,0:T(8,128)(2,1)}, bf16[272,256]{1,0:T(8,128)(2,1)S(1)}, u32[]{:S(2)}, u32[]{:S(2)}) collective-permute-start(bf16[272,256]{1,0:T(8,128)(2,1)} %get-tuple-element.25), channel_id=1, source_target_pairs={{0,80},{16,64},{32,112},{48,96},{64,16},{80,0},{96,48},{112,32},{1... | collective-permute-start | bytes 417800 | tf_op jit(solution)/shard_map/ppermute | solution.py:510
  62.1 10.9 %collective-permute-start.18 = (bf16[272,256]{1,0:T(8,128)(2,1)}, bf16[272,256]{1,0:T(8,128)(2,1)S(1)}, u32[]{:S(2)}, u32[]{:S(2)}) collective-permute-start(bf16[272,256]{1,0:T(8,128)(2,1)} %get-tuple-element.26), channel_id=1, source_target_pairs={{0,96},{16,112},{32,0},{48,16},{64,32},{80,48},{96,64},{112,80},{1... | collective-permute-start | bytes 417800 | tf_op jit(solution)/shard_map/ppermute | solution.py:510
  65.0 9.3 %collective-permute-start.19 = (bf16[272,256]{1,0:T(8,128)(2,1)}, bf16[272,256]{1,0:T(8,128)(2,1)}, u32[]{:S(2)}, u32[]{:S(2)}) collective-permute-start(bf16[272,256]{1,0:T(8,128)(2,1)} %get-tuple-element.27), channel_id=1, source_target_pairs={{0,112},{16,96},{32,16},{48,0},{64,48},{80,32},{96,80},{112,64},{1... | collective-permute-start | bytes 417800 | tf_op jit(solution)/shard_map/ppermute | solution.py:510
  83.9 35.8 %all-to-all-start.2 = ((bf16[16,256,128]{2,1,0:T(8,128)(2,1)}), bf16[16,256,128]{2,1,0:T(8,128)(2,1)}, u32[]{:S(2)}, u32[]{:S(2)}) async-start(bf16[16,256,128]{2,1,0:T(8,128)(2,1)} %shard_map.105), calls=%async_computation.2 | async-start | bytes 2097152 | tf_op jit(solution)/shard_map/all_to_all | solution.py:452
  (19 other events, 60.7 us)
